TPU v7x, 128 devices: a whole 4x4x4 slice. The times are simulated.
128 devices in a mesh: row: 32 (over z, y, core), col: 4 (over x).
Axes of the slice: x: 4, y: 4, z: 4, core: 2. Of those that a mesh axis runs over, the one named last changes fastest.
Arguments:
- rhs: bfloat16 [8, 32, 64, 128], P(None, 'row'), may hold values from -6 to 6
- boundary: bfloat16 [512, 64, 128], P('row'), may hold values from -6 to 6
- diag_inv: bfloat16 [8, 32, 128, 128], P(None, 'row'), may hold values from -0.5 to 0.5
- off_blocks: bfloat16 [7, 32, 128, 128, 128], P(None, 'row', 'col'), may hold values from -0.09375 to 0.09375
- coupling: int32 [7, 32, 128], P(None, 'row', 'col'), may hold values from 0 to 735, as said below
- present: int32 [7, 32, 128], P(None, 'row', 'col'), may hold values 0 or 1
Outputs:
- solution: bfloat16 [8, 32, 64, 128], P(None, 'row')
Inputs may be any that keep to these rules, and one draw needn't show every extreme that they name: coupling[l, q, k] is below 512 + (l + 1) * 32: it names a boundary block or a block of an earlier level; the slots of one block row name distinct blocks.
All inputs are finite; a program needn't handle non-finite values. No bound on the sum of `present` on one device may be relied on, other than what follows from the above.
Results may differ from a plain program's by a relative error of at most 0.012.
Values may be sent and summed in bfloat16 or wider, within the bound.
No kernel may reach another device: no remote copies, remote signals or barrier semaphores. Data moves between devices by JAX's collectives and lax.ppermute only.
A program may use at most 128 MiB of HBM per device.

v0:
```python
import jax
import jax.numpy as jnp
from jax import lax
from jax.sharding import PartitionSpec as P


def on_device(rhs, boundary, diag_inv, off_blocks, coupling, present):
    levels = rhs.shape[0]
    per_dev = rhs.shape[1]
    rhs_cols = rhs.shape[2]
    block = rhs.shape[3]
    row_count = lax.axis_size("row")
    width = per_dev * row_count
    outer_all = lax.all_gather(boundary, "row", axis=0, tiled=True)
    outer = outer_all.shape[0]
    empty = jnp.zeros((levels * width, rhs_cols, block), jnp.bfloat16)
    solved = jnp.concatenate([outer_all, empty], axis=0)
    results = []
    for level in range(levels):
        target = rhs[level].astype(jnp.float32)
        partial_value = None
        if level > 0:
            index = coupling[level - 1]
            slots = index.shape[1]
            picked = jnp.take(solved, index.reshape(-1), axis=0).reshape(
                per_dev, slots, rhs_cols, block
            )
            picked = picked * present[level - 1].astype(jnp.bfloat16)[:, :, None, None]
            partial_value = jnp.einsum(
                "ikab,ikrb->ira", off_blocks[level - 1], picked, preferred_element_type=jnp.float32
            )
        if level > 0:
            target = target - lax.psum(partial_value, "col")
        reduced = target.astype(jnp.bfloat16)
        own = jnp.einsum(
            "irb,iab->ira", reduced, diag_inv[level], preferred_element_type=jnp.float32
        ).astype(jnp.bfloat16)
        fresh = lax.all_gather(own, "row", axis=0, tiled=True)
        solved = solved.at[outer + level * width : outer + (level + 1) * width].set(fresh)
        results.append(own)
    return jnp.stack(results)


def solution(mesh):
    in_specs = (
        P(None, "row", None, None),
        P("row", None, None),
        P(None, "row", None, None),
        P(None, "row", "col", None, None),
        P(None, "row", "col"),
        P(None, "row", "col"),
    )
    out_specs = P(None, "row", None, None)
    return jax.shard_map(
        on_device, mesh=mesh, in_specs=in_specs, out_specs=out_specs, check_vma=False
    )
```

profile of v0, /device:TPU:1, one launch (start us, length us, event | category | flops | bytes accessed | tf_op | source)
XLA Modules:
  0.0 386.5 jit_solution(4677153188485968054)
XLA Ops:
  9.7 27.6 %all-gather = bf16[2048,128]{1,0:T(8,128)(2,1)S(1)} all-gather(bf16[64,128]{1,0:T(8,128)(2,1)S(1)} %get-tuple-element.124), channel_id=2, replica_groups=mesh['row'=32,'col'=4] {'row'}, dimensions={0}, use_global_device_ids=true | all-gather | bytes 540672 | tf_op jit(solution)/shard_map/all_gather | solution.py:38
  37.4 29.2 %all-gather.9.cloned.1.call-done = bf16[512,64,128]{2,1,0:T(8,128)(2,1)} async-done(((bf16[16,64,128]{2,1,0:T(8,128)(2,1)}), bf16[512,64,128]{2,1,0:T(8,128)(2,1)}) %all-gather.9.cloned.1.call-update) | async-done | bytes 8388624 | tf_op jit(solution)/shard_map/all_gather | solution.py:14
  66.5 10.5 %concatenate.17 = bf16[768,64,128]{2,1,0:T(8,128)(2,1)} pad(bf16[512,64,128]{2,1,0:T(8,128)(2,1)} %all-gather.9.cloned.1.call-done, bf16[]{:T(256)} %constant.200.clone.1), padding=0_256x0_0x0_0 | pad | bytes 20971522 | tf_op jit(solution)/shard_map/concatenate | solution.py:17
  77.9 5.2 %gather_fusion = bf16[32,64,128]{2,1,0:T(8,128)(2,1)S(1)} fusion(bf16[768,64,128]{2,1,0:T(8,128)(2,1)} %constant_dynamic-update-slice_fusion.13, s32[1024]{0:T(1024)S(1)} %pad_clamp_fusion.6), kind=kCustom, calls=%fused_computation.clone | custom fusion | bytes 1048704 | tf_op jit(solution)/shard_map/jit(_take)/gather | solution.py:25
  84.9 13.2 %psum.49 = f32[1,64,128]{2,1,0:T(8,128)S(1)} all-reduce(f32[1,64,128]{2,1,0:T(8,128)S(1)} %convolution_bitcast_fusion.6), channel_id=1, replica_groups=mesh['row'=32,'col'=4] {'col'}, use_global_device_ids=true, to_apply=%region_0.2 | all-reduce | flops 8192 | bytes 65536 | tf_op jit(solution)/shard_map/psum | solution.py:33
  98.3 28.3 %all-gather.1 = bf16[2048,128]{1,0:T(8,128)(2,1)S(1)} all-gather(bf16[64,128]{1,0:T(8,128)(2,1)S(1)} %get-tuple-element.126), channel_id=3, replica_groups=mesh['row'=32,'col'=4] {'row'}, dimensions={0}, use_global_device_ids=true | all-gather | bytes 540672 | tf_op jit(solution)/shard_map/all_gather | solution.py:38
  127.6 5.2 %gather_fusion.1 = bf16[32,64,128]{2,1,0:T(8,128)(2,1)S(1)} fusion(bf16[768,64,128]{2,1,0:T(8,128)(2,1)} %constant_dynamic-update-slice_fusion.12, s32[1024]{0:T(1024)S(1)} %pad_clamp_fusion.5), kind=kCustom, calls=%fused_computation.1.clone | custom fusion | bytes 1048704 | tf_op jit(solution)/shard_map/jit(_take)/gather | solution.py:25
  134.5 11.3 %psum.50 = f32[1,64,128]{2,1,0:T(8,128)S(1)} all-reduce(f32[1,64,128]{2,1,0:T(8,128)S(1)} %convolution_bitcast_fusion.5), channel_id=1, replica_groups=mesh['row'=32,'col'=4] {'col'}, use_global_device_ids=true, to_apply=%region_1.0 | all-reduce | flops 8192 | bytes 65536 | tf_op jit(solution)/shard_map/psum | solution.py:33
  146.0 25.7 %all-gather.2 = bf16[2048,128]{1,0:T(8,128)(2,1)S(1)} all-gather(bf16[64,128]{1,0:T(8,128)(2,1)S(1)} %get-tuple-element.128), channel_id=4, replica_groups=mesh['row'=32,'col'=4] {'row'}, dimensions={0}, use_global_device_ids=true | all-gather | bytes 540672 | tf_op jit(solution)/shard_map/all_gather | solution.py:38
  172.5 5.2 %gather_fusion.2 = bf16[32,64,128]{2,1,0:T(8,128)(2,1)S(1)} fusion(bf16[768,64,128]{2,1,0:T(8,128)(2,1)} %constant_dynamic-update-slice_fusion.11, s32[1024]{0:T(1024)S(1)} %pad_clamp_fusion.4), kind=kCustom, calls=%fused_computation.2.clone | custom fusion | bytes 1048704 | tf_op jit(solution)/shard_map/jit(_take)/gather | solution.py:25
  177.7 1.8 convolution_bitcast_fusion.4
  179.5 12.5 %psum.51 = f32[1,64,128]{2,1,0:T(8,128)S(1)} all-reduce(f32[1,64,128]{2,1,0:T(8,128)S(1)} %convolution_bitcast_fusion.4), channel_id=1, replica_groups=mesh['row'=32,'col'=4] {'col'}, use_global_device_ids=true, to_apply=%region_2.4 | all-reduce | flops 8192 | bytes 65536 | tf_op jit(solution)/shard_map/psum | solution.py:33
  192.2 27.9 %all-gather.3 = bf16[2048,128]{1,0:T(8,128)(2,1)S(1)} all-gather(bf16[64,128]{1,0:T(8,128)(2,1)S(1)} %get-tuple-element.130), channel_id=5, replica_groups=mesh['row'=32,'col'=4] {'row'}, dimensions={0}, use_global_device_ids=true | all-gather | bytes 540672 | tf_op jit(solution)/shard_map/all_gather | solution.py:38
  220.9 5.2 %gather_fusion.3 = bf16[32,64,128]{2,1,0:T(8,128)(2,1)S(1)} fusion(bf16[768,64,128]{2,1,0:T(8,128)(2,1)} %constant_dynamic-update-slice_fusion.10, s32[1024]{0:T(1024)S(1)} %pad_clamp_fusion.3), kind=kCustom, calls=%fused_computation.3.clone | custom fusion | bytes 1048704 | tf_op jit(solution)/shard_map/jit(_take)/gather | solution.py:25
  227.9 11.3 %psum.52 = f32[1,64,128]{2,1,0:T(8,128)S(1)} all-reduce(f32[1,64,128]{2,1,0:T(8,128)S(1)} %convolution_bitcast_fusion.3), channel_id=1, replica_groups=mesh['row'=32,'col'=4] {'col'}, use_global_device_ids=true, to_apply=%region_3.5 | all-reduce | flops 8192 | bytes 65536 | tf_op jit(solution)/shard_map/psum | solution.py:33
  239.3 25.9 %all-gather.4 = bf16[2048,128]{1,0:T(8,128)(2,1)S(1)} all-gather(bf16[64,128]{1,0:T(8,128)(2,1)S(1)} %get-tuple-element.132), channel_id=6, replica_groups=mesh['row'=32,'col'=4] {'row'}, dimensions={0}, use_global_device_ids=true | all-gather | bytes 540672 | tf_op jit(solution)/shard_map/all_gather | solution.py:38
  266.1 5.2 %gather_fusion.4 = bf16[32,64,128]{2,1,0:T(8,128)(2,1)S(1)} fusion(bf16[768,64,128]{2,1,0:T(8,128)(2,1)} %constant_dynamic-update-slice_fusion.9, s32[1024]{0:T(1024)S(1)} %pad_clamp_fusion.2), kind=kCustom, calls=%fused_computation.4.clone | custom fusion | bytes 1048704 | tf_op jit(solution)/shard_map/jit(_take)/gather | solution.py:25
  273.1 12.5 %psum.53 = f32[1,64,128]{2,1,0:T(8,128)S(1)} all-reduce(f32[1,64,128]{2,1,0:T(8,128)S(1)} %convolution_bitcast_fusion.2), channel_id=1, replica_groups=mesh['row'=32,'col'=4] {'col'}, use_global_device_ids=true, to_apply=%region_4.6 | all-reduce | flops 8192 | bytes 65536 | tf_op jit(solution)/shard_map/psum | solution.py:33
  285.7 27.9 %all-gather.5 = bf16[2048,128]{1,0:T(8,128)(2,1)S(1)} all-gather(bf16[64,128]{1,0:T(8,128)(2,1)S(1)} %get-tuple-element.134), channel_id=7, replica_groups=mesh['row'=32,'col'=4] {'row'}, dimensions={0}, use_global_device_ids=true | all-gather | bytes 540672 | tf_op jit(solution)/shard_map/all_gather | solution.py:38
  314.5 5.2 %gather_fusion.5 = bf16[32,64,128]{2,1,0:T(8,128)(2,1)S(1)} fusion(bf16[768,64,128]{2,1,0:T(8,128)(2,1)} %constant_dynamic-update-slice_fusion.8, s32[1024]{0:T(1024)S(1)} %pad_clamp_fusion.1), kind=kCustom, calls=%fused_computation.5.clone | custom fusion | bytes 1048704 | tf_op jit(solution)/shard_map/jit(_take)/gather | solution.py:25
  321.5 11.3 %psum.54 = f32[1,64,128]{2,1,0:T(8,128)S(1)} all-reduce(f32[1,64,128]{2,1,0:T(8,128)S(1)} %convolution_bitcast_fusion.1), channel_id=1, replica_groups=mesh['row'=32,'col'=4] {'col'}, use_global_device_ids=true, to_apply=%region_5.7 | all-reduce | flops 8192 | bytes 65536 | tf_op jit(solution)/shard_map/psum | solution.py:33
  332.9 25.7 %all-gather.6 = bf16[2048,128]{1,0:T(8,128)(2,1)S(1)} all-gather(bf16[64,128]{1,0:T(8,128)(2,1)S(1)} %get-tuple-element.136), channel_id=8, replica_groups=mesh['row'=32,'col'=4] {'row'}, dimensions={0}, use_global_device_ids=true | all-gather | bytes 540672 | tf_op jit(solution)/shard_map/all_gather | solution.py:38
  359.4 5.2 %gather_fusion.6 = bf16[32,64,128]{2,1,0:T(8,128)(2,1)S(1)} fusion(bf16[768,64,128]{2,1,0:T(8,128)(2,1)} %constant_dynamic-update-slice_fusion.7, s32[1024]{0:T(1024)S(1)} %pad_clamp_fusion), kind=kCustom, calls=%fused_computation.6.clone | custom fusion | bytes 1048704 | tf_op jit(solution)/shard_map/jit(_take)/gather | solution.py:25
  366.4 12.5 %psum.55 = f32[1,64,128]{2,1,0:T(8,128)S(1)} all-reduce(f32[1,64,128]{2,1,0:T(8,128)S(1)} %convolution_bitcast_fusion), channel_id=1, replica_groups=mesh['row'=32,'col'=4] {'col'}, use_global_device_ids=true, to_apply=%region_6.8 | all-reduce | flops 8192 | bytes 65536 | tf_op jit(solution)/shard_map/psum | solution.py:33
  (39 shorter events, 21.3 us)
Async XLA Ops:
  6.5 60.0 %all-gather.9.cloned.1.call-start = ((), (), s32[]{:S(2)}) async-start(), calls=%async_computation | async-start | bytes 8650752 | tf_op jit(solution)/shard_map/all_gather | solution.py:14
  37.3 60.8 %copy-start = (bf16[8,1,128,128]{3,2,1,0:T(8,128)(2,1)S(1)}, bf16[8,1,128,128]{3,2,1,0:T(8,128)(2,1)}, u32[]{:S(2)}) copy-start(bf16[8,1,128,128]{3,2,1,0:T(8,128)(2,1)} %param.24) | copy-start | bytes 786436
  37.4 60.8 %copy-start.1 = (bf16[8,1,64,128]{3,2,1,0:T(8,128)(2,1)S(1)}, bf16[8,1,64,128]{3,2,1,0:T(8,128)(2,1)}, u32[]{:S(2)}) copy-start(bf16[8,1,64,128]{3,2,1,0:T(8,128)(2,1)} %param.22) | copy-start | bytes 393220
  332.9 46.0 %copy-start.2 = (bf16[8,1,64,128]{3,2,1,0:T(8,128)(2,1)}, bf16[8,1,64,128]{3,2,1,0:T(8,128)(2,1)S(1)}, u32[]{:S(2)}) copy-start(bf16[8,1,64,128]{3,2,1,0:T(8,128)(2,1)S(1)} %get-tuple-element.135) | copy-start | bytes 393220
Sparse Core Ops, SparseCore 0:
  9.6 56.8 all-gather.8
where the time goes:
time: 390 us; the launch traced here: 387 us
  blocking collectives  274 us (70%)
  local copies, waits for them, and re-layouts  53.1 us (14%)
  waiting for transfers between devices  29.9 us (8%)
  matrix products  14.8 us (4%)
  between operations  13.7 us (4%)
    all_gather x7, blocking collectives, on_device(): fresh = lax.all_gather(own, 'row', axis=0, tiled=True)  189 us
    psum x7, blocking collectives, on_device(): target = target - lax.psum(partial_value, 'col')  84.6 us
    gather x7, local copies, waits for them, and re-layouts, on_device(): jnp.take(solved, index.reshape(-1), axis=0)  36.6 us
    all_gather x1, waiting for transfers between devices, on_device(): outer_all = lax.all_gather(boundary, 'row', axis=0, tiled=True)  29.2 us
    dot_general x7, matrix products, on_device(): jnp.einsum('ikab,ikrb->ira', off_blocks[level - 1], picked, preferred_ele...  12.3 us
    concatenate x1, local copies, waits for them, and re-layouts, on_device(): solved = jnp.concatenate([outer_all, empty], axis=0)  10.5 us
  transfers between devices with their start and end apart: 1, of which 1 were waited for; matrix products, arithmetic and copies ran while one was open for 1% of the time, Pallas kernels for 0%

commit v1 on v0

v1 whole, which is shorter than its diff:
```python
import jax
import jax.numpy as jnp
from jax import lax
from jax.experimental import pallas as pl
from jax.experimental.pallas import tpu as pltpu
from jax.sharding import Mesh, PartitionSpec as P

ROWS = ("z", "y", "core")
VMEM_LIMIT = 48 * 1024 * 1024


def xor_pairs(n, k):
    return [(i, i ^ k) for i in range(n)]


def shift_pairs(n, k):
    return [(i, (i + k) % n) for i in range(n)]


def swap_cores(v):
    return lax.ppermute(v, "core", xor_pairs(2, 1))


def direct_gather(v, axis):
    return jnp.concatenate([v] + [lax.ppermute(v, axis, xor_pairs(4, k)) for k in (1, 2, 3)])


def ring_gather(v, axis):
    before = lax.ppermute(v, axis, shift_pairs(4, 1))
    after = lax.ppermute(v, axis, shift_pairs(4, 3))
    half = v.shape[0] // 2
    far_a = lax.ppermute(before[:half], axis, shift_pairs(4, 1))
    far_b = lax.ppermute(after[half:], axis, shift_pairs(4, 3))
    return jnp.concatenate([v, before, after, far_a, far_b])


def nt_dot(x, a):
    return lax.dot_general(x, a, (((1,), (1,)), ((), ())), preferred_element_type=jnp.float32)


GROUP = 8


def old_kernel(code_ref, *refs):
    sources, (own_ref, other_ref, out_ref, picked, sem) = refs[:-5], refs[-5:]
    slots = code_ref.shape[0]

    for k in range(slots):
        code = jnp.maximum(code_ref[k], 0)
        which, place = code // 1024, code % 1024
        if len(sources) == 1:
            pltpu.make_async_copy(sources[0].at[place], picked.at[k], sem).start()
        else:
            for s, source in enumerate(sources):

                @pl.when(which == s)
                def _(source=source, k=k, place=place):
                    pltpu.make_async_copy(source.at[place], picked.at[k], sem).start()

    pltpu.make_async_copy(sources[0].at[pl.ds(0, slots)], picked, sem).wait()
    per_row = slots // 2
    for r, a_ref in enumerate((own_ref, other_ref)):
        total = None
        for g in range(0, per_row, GROUP):
            xs, blocks = [], []
            for k in range(g, g + GROUP):
                kept = (code_ref[r * per_row + k] >= 0).astype(jnp.float32)
                xs.append((picked[r * per_row + k].astype(jnp.float32) * kept).astype(jnp.bfloat16))
                blocks.append(a_ref[0, 0, k])
            part = nt_dot(jnp.concatenate(xs, axis=1), jnp.concatenate(blocks, axis=1))
            total = part if total is None else total + part
        out_ref[r] = total


def old_sum(level, code, sources, own, other):
    slots, (rhs_cols, block) = code.shape[0], sources[0].shape[1:]
    per_row = slots // 2
    a_spec = pl.BlockSpec((1, 1, per_row, block, block), lambda i: (level - 1, 0, 0, 0, 0))
    return pl.pallas_call(
        old_kernel,
        grid=(1,),
        out_shape=jax.ShapeDtypeStruct((2, rhs_cols, block), jnp.float32),
        in_specs=[pl.BlockSpec(memory_space=pltpu.SMEM)]
        + [pl.BlockSpec(memory_space=pl.ANY)] * len(sources)
        + [a_spec, a_spec],
        out_specs=pl.BlockSpec((2, rhs_cols, block), lambda i: (0, 0, 0)),
        scratch_shapes=[pltpu.VMEM((slots, rhs_cols, block), jnp.bfloat16), pltpu.SemaphoreType.DMA],
        compiler_params=pltpu.CompilerParams(vmem_limit_bytes=VMEM_LIMIT),
        cost_estimate=pl.CostEstimate(
            flops=2 * slots * rhs_cols * block * block,
            bytes_accessed=slots * block * (block + 2 * rhs_cols) * 4,
            transcendentals=0,
        ),
        name="old_sum",
    )(code, *sources, own, other)


def fresh_kernel(code_ref, x_ref, old_ref, own_ref, other_ref, out_ref):
    per_row = code_ref.shape[0] // 2
    for r, a_ref in enumerate((own_ref, other_ref)):
        out_ref[r] = old_ref[r]

        def add(k, carry, r=r, a_ref=a_ref):
            code = code_ref[r * per_row + k]

            @pl.when(code >= 0)
            def _():
                out_ref[r] += nt_dot(x_ref[code], a_ref[0, 0, k])

            return carry

        lax.fori_loop(0, per_row, add, 0)


def fresh_sum(level, code, solved, old, own, other):
    slots, (rhs_cols, block) = code.shape[0], solved.shape[1:]
    per_row = slots // 2
    a_spec = pl.BlockSpec((1, 1, per_row, block, block), lambda i: (level - 1, 0, 0, 0, 0))
    whole = lambda shape: pl.BlockSpec(shape, lambda i: (0,) * len(shape))
    return pl.pallas_call(
        fresh_kernel,
        grid=(1,),
        out_shape=jax.ShapeDtypeStruct(old.shape, jnp.float32),
        in_specs=[pl.BlockSpec(memory_space=pltpu.SMEM), whole(solved.shape), whole(old.shape), a_spec, a_spec],
        out_specs=whole(old.shape),
        compiler_params=pltpu.CompilerParams(vmem_limit_bytes=VMEM_LIMIT),
        cost_estimate=pl.CostEstimate(
            flops=2 * 8 * rhs_cols * block * block, bytes_accessed=slots * block * block * 2, transcendentals=0
        ),
        name="fresh_sum",
    )(code, solved, old, own, other)


def solve_kernel(core_ref, p0, p1, p2, p3, rhs_ref, own_d_ref, other_d_ref, out_ref, all_ref):
    core = core_ref[0]
    for r, d_ref in enumerate((own_d_ref, other_d_ref)):
        coupled = (p0[r] + p1[r]) + (p2[r] + p3[r])
        reduced = (rhs_ref[0, r].astype(jnp.float32) - coupled).astype(jnp.bfloat16)
        solved = nt_dot(reduced, d_ref[0, 0]).astype(jnp.bfloat16)
        out_ref[r] = solved
        if all_ref is not None:
            row = core ^ r
            for i in range(all_ref.shape[0]):
                all_ref[i, row] = solved


def solve_level(level, core, partials, rhs, own_d, other_d, copies):
    _, rhs_cols, block = partials[0].shape
    whole = lambda shape: pl.BlockSpec(shape, lambda i: (0,) * len(shape))
    d_spec = pl.BlockSpec((1, 1, block, block), lambda i: (level, 0, 0, 0))
    d2_spec = pl.BlockSpec((1, 1, block, block), lambda i: (level, 0, 0, 0))
    out_shape = [jax.ShapeDtypeStruct((2, rhs_cols, block), jnp.bfloat16)]
    if copies:
        out_shape.append(jax.ShapeDtypeStruct((copies, 2, rhs_cols, block), jnp.bfloat16))
        body = solve_kernel
    else:
        body = lambda *refs: solve_kernel(*refs, None)
    return pl.pallas_call(
        body,
        grid=(1,),
        out_shape=out_shape,
        in_specs=[pl.BlockSpec(memory_space=pltpu.SMEM)]
        + [whole(partials[0].shape)] * 4
        + [pl.BlockSpec((1, 2, rhs_cols, block), lambda i: (level, 0, 0, 0)), d_spec, d2_spec],
        out_specs=[whole(s.shape) for s in out_shape],
        compiler_params=pltpu.CompilerParams(vmem_limit_bytes=VMEM_LIMIT),
        name="solve_level",
    )(core, *partials, rhs, own_d, other_d)


def on_device(rhs, boundary, diag_inv, off_blocks, coupling, present):
    levels, _, rhs_cols, block = rhs.shape
    outer_each = boundary.shape[0]
    outer = outer_each * 32
    half = rhs_cols // 2
    z, y, core = lax.axis_index("z"), lax.axis_index("y"), lax.axis_index("core")

    def my_half(v, axis):
        return lax.dynamic_slice_in_dim(v, core * half, half, axis)

    def their_half(v, axis):
        return lax.dynamic_slice_in_dim(v, (1 - core) * half, half, axis)

    first = jnp.einsum("rb,ab->ra", rhs[0, 0], diag_inv[0, 0], preferred_element_type=jnp.float32).astype(jnp.bfloat16)
    known = jnp.concatenate([boundary, first[None]])
    known_own = my_half(known, 1)
    known_other = swap_cores(their_half(known, 1))
    color_a = ring_gather(direct_gather(known_own, "z"), "y")
    color_b = ring_gather(direct_gather(known_other, "y"), "z")
    store = jnp.concatenate([color_a, color_b])

    code_own = (coupling + 1024 * present)[:, 0]
    code_both = jnp.stack([code_own, swap_cores(code_own)], axis=1)
    rhs_both = jnp.concatenate([my_half(rhs, 2), swap_cores(their_half(rhs, 2))], axis=1)
    diag_other = swap_cores(diag_inv)
    off_other = swap_cores(off_blocks)

    keep, index = code_both >= 1024, code_both % 1024
    in_outer = index < outer
    row = jnp.where(in_outer, index // outer_each, index - outer)
    member = jnp.where(in_outer, index % outer_each, outer_each)
    src_z, src_y, src_core = row // 8, (row // 2) % 4, row % 2
    each = outer_each + 1
    ring_place = lambda d: jnp.where(d == 3, 1, jnp.where(d == 1, 2, jnp.where(d == 2, 3, 0)))
    place_a = ring_place((src_y - y) % 4) * 4 + (src_z ^ z)
    place_b = 16 + ring_place((src_z - z) % 4) * 4 + (src_y ^ y)
    place_known = jnp.where(src_core == core, place_a, place_b) * each + member
    level_of = jnp.maximum(index - outer, 0) // 32
    code = jnp.where(level_of == 0, place_known, level_of * 1024 + (index - outer) % 32)
    this = jnp.arange(levels - 1)[:, None, None]
    is_fresh = (level_of == this) & (level_of > 0)
    old_code = jnp.where(keep & ~is_fresh, code, -1).reshape(levels - 1, -1)
    fresh_code = jnp.where(keep & is_fresh, code % 1024, -1).reshape(levels - 1, -1)

    core_arr = jnp.reshape(core, (1,)).astype(jnp.int32)
    sources = [store]
    own_rows, other_rows = [], []
    value = old_sum(1, old_code[0], sources, off_blocks, off_other)
    for level in range(1, levels):
        partials = [value] + [lax.ppermute(value, "x", xor_pairs(4, k)) for k in (1, 2, 3)]
        last = level == levels - 1
        if not last:
            next_code, value = lax.optimization_barrier((old_code[level], value))
            old = old_sum(level + 1, next_code, sources, off_blocks, off_other)
        outs = solve_level(level, core_arr, partials, rhs_both, diag_inv, diag_other, 0 if last else 16)
        own_rows.append(outs[0][0])
        other_rows.append(outs[0][1])
        if not last:
            solved = lax.all_to_all(outs[1], ("z", "y"), 0, 0).reshape(32, half, block)
            value = fresh_sum(level + 1, fresh_code[level], solved, old, off_blocks, off_other)
            sources = sources + [solved]

    mine = jnp.stack(own_rows)
    theirs = swap_cores(jnp.stack(other_rows))
    low = jnp.where(core == 0, mine, theirs)
    high = jnp.where(core == 0, theirs, mine)
    rest = jnp.concatenate([low, high], axis=1)
    return jnp.concatenate([first[None], rest])[:, None]


def solution(mesh):
    split = Mesh(mesh.devices.reshape(4, 4, 2, 4), ("z", "y", "core", "x"))
    in_specs = (
        P(None, ROWS, None, None),
        P(ROWS, None, None),
        P(None, ROWS, None, None),
        P(None, ROWS, "x", None, None),
        P(None, ROWS, "x"),
        P(None, ROWS, "x"),
    )
    return jax.shard_map(
        on_device, mesh=split, in_specs=in_specs, out_specs=P(None, ROWS, None, None), check_vma=False
    )
```

time: 390 us -> 244 us (0.63)
  blocking collectives: 274 us -> 0 us
  starting transfers between devices: 0.01 us -> 97.7 us
  Pallas kernels: 0 us -> 52.2 us
  waiting for transfers between devices: 29.9 us -> 76.1 us
  local copies, waits for them, and re-layouts: 53.1 us -> 12.4 us
  matrix products: 14.8 us -> 0.9 us
  between operations: 13.7 us -> 0.37 us
    all_gather x7 -> x0, blocking collectives: 189 us -> none  [on_device(): fresh = lax.all_gather(own, 'row', axis=0, tiled=True)]
    psum x7 -> x0, blocking collectives: 84.6 us -> none  [on_device(): target = target - lax.psum(partial_value, 'col')]
    ppermute x0 -> x41, starting transfers between devices: none -> 72.4 us  [the longest x21 27.5 us: on_device(): lax.ppermute(value, 'x', xor_pairs(4, k))]
    ppermute x0 -> x41, waiting for transfers between devices: none -> 59.3 us  [the longest x21 18.6 us: on_device(): lax.ppermute(value, 'x', xor_pairs(4, k))]
    pallas_call x0 -> x20, Pallas kernels: none -> 52.2 us  [the longest x7 31.5 us: old_sum(): pl.pallas_call(old_kernel, grid=(1,), out_shape=jax.ShapeDtypeStruct((2,...]
    gather x7 -> x0, local copies, waits for them, and re-layouts: 36.6 us -> none  [on_device(): jnp.take(solved, index.reshape(-1), axis=0)]
    all_gather x1 -> x0, waiting for transfers between devices: 29.2 us -> none  [on_device(): outer_all = lax.all_gather(boundary, 'row', axis=0, tiled=True)]
    all_to_all x0 -> x6, starting transfers between devices: none -> 25.2 us  [on_device(): solved = lax.all_to_all(outs[1], ('z', 'y'), 0, 0).reshape(32, half, block)]
  transfers between devices with their start and end apart: 1 -> 47, of which waited for: 1 -> 33; matrix products, arithmetic and copies ran while one was open for 1% -> 6% of each run, Pallas kernels for 0% -> 13%
where the time goes in v1:
time: 244 us; the launch traced here: 242 us
  starting transfers between devices  97.7 us (40%)
  waiting for transfers between devices  76.1 us (31%)
  Pallas kernels  52.2 us (21%)
  local copies, waits for them, and re-layouts  12.4 us (5%)
  other arithmetic  2.68 us (1%)
    pallas_call x7, Pallas kernels, old_sum(): pl.pallas_call(old_kernel, grid=(1,), out_shape=jax.ShapeDtypeStruct((2,...  31.5 us
    ppermute x21, starting transfers between devices, on_device(): lax.ppermute(value, 'x', xor_pairs(4, k))  27.5 us
    ppermute x6, starting transfers between devices, swap_cores(): return lax.ppermute(v, 'core', xor_pairs(2, 1))  26.4 us
    all_to_all x6, starting transfers between devices, on_device(): solved = lax.all_to_all(outs[1], ('z', 'y'), 0, 0).reshape(32, half, block)  25.2 us
    ppermute x21, waiting for transfers between devices, on_device(): lax.ppermute(value, 'x', xor_pairs(4, k))  18.6 us
    all_to_all x6, waiting for transfers between devices, on_device(): solved = lax.all_to_all(outs[1], ('z', 'y'), 0, 0).reshape(32, half, block)  16.9 us
    pallas_call x6, Pallas kernels, fresh_sum(): pl.pallas_call(fresh_kernel, grid=(1,), out_shape=jax.ShapeDtypeStruct(ol...  15.3 us
    ppermute x2, waiting for transfers between devices, ring_gather(): before = lax.ppermute(v, axis, shift_pairs(4, 1))  13.3 us
  transfers between devices with their start and end apart: 47, of which 33 were waited for; matrix products, arithmetic and copies ran while one was open for 6% of the time, Pallas kernels for 13%

profile of v1, /device:TPU:1, one launch (start us, length us, event | category | flops | bytes accessed | tf_op | source)
XLA Modules:
  0.0 242.4 jit_solution(13568809262290188345)
XLA Ops:
  5.8 3.3 %collective-permute-start.2 = (bf16[17,32,128]{2,1,0:T(8,128)(2,1)S(1)}, bf16[17,32,128]{2,1,0:T(8,128)(2,1)S(1)}, u32[]{:S(2)}, u32[]{:S(2)}) collective-permute-start(bf16[17,32,128]{2,1,0:T(8,128)(2,1)S(1)} %get-tuple-element.45), channel_id=1, source_target_pairs={{0,64},{32,96},{64,0},{96,32},{1,65},{33,97},{65,1},{97,33},{2,66}... | collective-permute-start | bytes 417800 | tf_op jit(solution)/shard_map/ppermute | solution.py:25
  9.8 6.1 %collective-permute-done.2 = bf16[17,32,128]{2,1,0:T(8,128)(2,1)S(1)} collective-permute-done((bf16[17,32,128]{2,1,0:T(8,128)(2,1)S(1)}, bf16[17,32,128]{2,1,0:T(8,128)(2,1)S(1)}, u32[]{:S(2)}, u32[]{:S(2)}) %collective-permute-start.2) | collective-permute-done | bytes 139296 | tf_op jit(solution)/shard_map/ppermute | solution.py:25
  24.1 9.2 %collective-permute-done.4 = bf16[68,32,128]{2,1,0:T(8,128)(2,1)S(1)} collective-permute-done((bf16[68,32,128]{2,1,0:T(8,128)(2,1)S(1)}, bf16[68,32,128]{2,1,0:T(8,128)(2,1)S(1)}, u32[]{:S(2)}, u32[]{:S(2)}) %collective-permute-start.4) | collective-permute-done | bytes 557088 | tf_op jit(solution)/shard_map/ppermute | solution.py:29
  51.0 3.6 %collective-permute-start = (s32[7,32]{1,0:T(8,128)S(1)}, s32[7,32]{1,0:T(8,128)S(1)}, u32[]{:S(2)}, u32[]{:S(2)}) collective-permute-start(s32[7,32]{1,0:T(8,128)S(1)} %bitcast.43), channel_id=1, source_target_pairs={{0,4},{4,0},{1,5},{5,1},{2,6},{6,2},{3,7},{7,3},{8,12},{12,8},{9,1... | collective-permute-start | bytes 2696 | tf_op jit(solution)/shard_map/ppermute | solution.py:21
  58.7 4.1 %collective-permute-done.12 = bf16[68,32,128]{2,1,0:T(8,128)(2,1)S(1)} collective-permute-done((bf16[68,32,128]{2,1,0:T(8,128)(2,1)S(1)}, bf16[68,32,128]{2,1,0:T(8,128)(2,1)S(1)}, u32[]{:S(2)}, u32[]{:S(2)}) %collective-permute-start.12) | collective-permute-done | bytes 557088 | tf_op jit(solution)/shard_map/ppermute | solution.py:29
  63.0 7.1 %collective-permute-done.13 = bf16[68,32,128]{2,1,0:T(8,128)(2,1)S(1)} collective-permute-done((bf16[68,32,128]{2,1,0:T(8,128)(2,1)S(1)}, bf16[68,32,128]{2,1,0:T(8,128)(2,1)S(1)}, u32[]{:S(2)}, u32[]{:S(2)}) %collective-permute-start.13) | collective-permute-done | bytes 557088 | tf_op jit(solution)/shard_map/ppermute | solution.py:30
  70.1 3.5 %collective-permute-start.15 = (bf16[34,32,128]{2,1,0:T(8,128)(2,1)S(1)}, bf16[34,32,128]{2,1,0:T(8,128)(2,1)S(1)}, u32[]{:S(2)}, u32[]{:S(2)}) collective-permute-start(bf16[34,32,128]{2,1,0:T(8,128)(2,1)S(1)} %slice.149), channel_id=1, source_target_pairs={{0,96},{32,0},{64,32},{96,64},{1,97},{33,1},{65,33},{97,65},{2,98}... | collective-permute-start | bytes 835592 | tf_op jit(solution)/shard_map/ppermute | solution.py:33
  79.1 3.9 %old_sum.7.p0 = f32[2,32,128]{2,1,0:T(8,128)S(1)} custom-call(s32[64]{0:T(128)S(1)} %squeeze.51.code_ref, bf16[544,32,128]{2,1,0:T(8,128)(2,1)} %constant_dynamic-update-slice_fusion.4.refs_0_, bf16[7,1,32,128,128]{4,3,2,1,0:T(8,128)(2,1)} %own_ref.11, ...), custom_call_target="tpu_custom_call" | custom-call | flops 67108864 | bytes 6291456 | tf_op jit(solution)/shard_map/old_sum/pallas_call | solution.py:79
  91.3 6.2 %all-to-all-start = ((bf16[16,2,32,128]{3,2,1,0:T(8,128)(2,1)}), bf16[16,2,32,128]{3,2,1,0:T(8,128)(2,1)S(1)}, u32[]{:S(2)}, u32[]{:S(2)}) async-start(bf16[16,2,32,128]{3,2,1,0:T(8,128)(2,1)} %get-tuple-element.24), calls=%async_computation | async-start | bytes 524288 | tf_op jit(solution)/shard_map/all_to_all | solution.py:229
  97.8 4.0 %old_sum.8.old_ref = f32[2,32,128]{2,1,0:T(8,128)S(1)} custom-call(s32[64]{0:T(128)S(1)} %squeeze.53.code_ref, bf16[544,32,128]{2,1,0:T(8,128)(2,1)} %constant_dynamic-update-slice_fusion.4.refs_0_, bf16[7,1,32,128,128]{4,3,2,1,0:T(8,128)(2,1)} %own_ref.11, ...), custom_call_target="tpu_custom_call" | custom-call | flops 67108864 | bytes 6291456 | tf_op jit(solution)/shard_map/old_sum/pallas_call | solution.py:79
  101.7 3.4 %all-to-all-done = bf16[16,2,32,128]{3,2,1,0:T(8,128)(2,1)S(1)} async-done(((bf16[16,2,32,128]{3,2,1,0:T(8,128)(2,1)}), bf16[16,2,32,128]{3,2,1,0:T(8,128)(2,1)S(1)}, u32[]{:S(2)}, u32[]{:S(2)}) %all-to-all-start) | async-done | bytes 262176 | tf_op jit(solution)/shard_map/all_to_all | solution.py:229
  113.9 3.5 %all-to-all-start.1 = ((bf16[16,2,32,128]{3,2,1,0:T(8,128)(2,1)}), bf16[16,2,32,128]{3,2,1,0:T(8,128)(2,1)S(1)}, u32[]{:S(2)}, u32[]{:S(2)}) async-start(bf16[16,2,32,128]{3,2,1,0:T(8,128)(2,1)} %get-tuple-element.27), calls=%async_computation.1 | async-start | bytes 524288 | tf_op jit(solution)/shard_map/all_to_all | solution.py:229
  117.6 4.1 %old_sum.9.old_ref = f32[2,32,128]{2,1,0:T(8,128)S(1)} custom-call(s32[64]{0:T(128)S(1)} %squeeze.55.code_ref, bf16[544,32,128]{2,1,0:T(8,128)(2,1)} %constant_dynamic-update-slice_fusion.4.refs_0_, bf16[32,32,128]{2,1,0:T(8,128)(2,1)S(1)} %bitcast.23, bf16[7,1,32,128,128]{4,3,2,1,0:T(8,128)(2,1)} %own_ref.11, ...), custom_call_target="tpu_custom_call" | custom-call | flops 67108864 | bytes 6291456 | tf_op jit(solution)/shard_map/old_sum/pallas_call | solution.py:79
  121.7 3.3 %all-to-all-done.1 = bf16[16,2,32,128]{3,2,1,0:T(8,128)(2,1)S(1)} async-done(((bf16[16,2,32,128]{3,2,1,0:T(8,128)(2,1)}), bf16[16,2,32,128]{3,2,1,0:T(8,128)(2,1)S(1)}, u32[]{:S(2)}, u32[]{:S(2)}) %all-to-all-start.1) | async-done | bytes 262176 | tf_op jit(solution)/shard_map/all_to_all | solution.py:229
  128.3 3.1 %collective-permute-start.26 = (f32[2,32,128]{2,1,0:T(8,128)S(1)}, f32[2,32,128]{2,1,0:T(8,128)S(1)}, u32[]{:S(2)}, u32[]{:S(2)}) collective-permute-start(f32[2,32,128]{2,1,0:T(8,128)S(1)} %fresh_sum.7.p0), channel_id=1, source_target_pairs={{0,2},{1,3},{2,0},{3,1},{4,6},{5,7},{6,4},{7,5},{8,10},{9,11},{10,... | collective-permute-start | bytes 98312 | tf_op jit(solution)/shard_map/ppermute | solution.py:220
  136.2 3.5 %all-to-all-start.2 = ((bf16[16,2,32,128]{3,2,1,0:T(8,128)(2,1)}), bf16[16,2,32,128]{3,2,1,0:T(8,128)(2,1)S(1)}, u32[]{:S(2)}, u32[]{:S(2)}) async-start(bf16[16,2,32,128]{3,2,1,0:T(8,128)(2,1)} %get-tuple-element.30), calls=%async_computation.2 | async-start | bytes 524288 | tf_op jit(solution)/shard_map/all_to_all | solution.py:229
  139.9 4.3 %old_sum.10.old_ref = f32[2,32,128]{2,1,0:T(8,128)S(1)} custom-call(s32[64]{0:T(128)S(1)} %squeeze.57.code_ref, bf16[544,32,128]{2,1,0:T(8,128)(2,1)} %constant_dynamic-update-slice_fusion.4.refs_0_, bf16[32,32,128]{2,1,0:T(8,128)(2,1)S(1)} %bitcast.24, bf16[32,32,128]{2,1,0:T(8,128)(2,1)S(1)} %bitcast.29, bf16[7,1,32,128,128]{4,3,2,1,0:T(8,128)(2,1)} %own_ref.11, ...), custom_call_target="tpu_custom_call" | custom-call | flops 67108864 | bytes 6291456 | tf_op jit(solution)/shard_map/old_sum/pallas_call | solution.py:79
  156.4 3.8 %all-to-all-start.3 = ((bf16[16,2,32,128]{3,2,1,0:T(8,128)(2,1)}), bf16[16,2,32,128]{3,2,1,0:T(8,128)(2,1)S(1)}, u32[]{:S(2)}, u32[]{:S(2)}) async-start(bf16[16,2,32,128]{3,2,1,0:T(8,128)(2,1)} %get-tuple-element.33), calls=%async_computation.3 | async-start | bytes 524288 | tf_op jit(solution)/shard_map/all_to_all | solution.py:229
  160.4 4.6 %old_sum.11.old_ref = f32[2,32,128]{2,1,0:T(8,128)S(1)} custom-call(s32[64]{0:T(128)S(1)} %squeeze.59.code_ref, bf16[544,32,128]{2,1,0:T(8,128)(2,1)} %constant_dynamic-update-slice_fusion.4.refs_0_, bf16[32,32,128]{2,1,0:T(8,128)(2,1)S(1)} %bitcast.25, bf16[32,32,128]{2,1,0:T(8,128)(2,1)S(1)} %bitcast.30, bf16[32,32,128]{2,1,0:T(8,128)(2,1)S(1)} %bitcast.34, ...), custom_call_target="tpu_custom_call" | custom-call | flops 67108864 | bytes 6291456 | tf_op jit(solution)/shard_map/old_sum/pallas_call | solution.py:79
  178.5 3.9 %all-to-all-start.4 = ((bf16[16,2,32,128]{3,2,1,0:T(8,128)(2,1)}), bf16[16,2,32,128]{3,2,1,0:T(8,128)(2,1)S(1)}, u32[]{:S(2)}, u32[]{:S(2)}) async-start(bf16[16,2,32,128]{3,2,1,0:T(8,128)(2,1)} %get-tuple-element.36), calls=%async_computation.4 | async-start | bytes 524288 | tf_op jit(solution)/shard_map/all_to_all | solution.py:229
  182.4 5.0 %old_sum.12.old_ref = f32[2,32,128]{2,1,0:T(8,128)S(1)} custom-call(s32[64]{0:T(128)S(1)} %squeeze.61.code_ref, bf16[544,32,128]{2,1,0:T(8,128)(2,1)} %constant_dynamic-update-slice_fusion.4.refs_0_, bf16[32,32,128]{2,1,0:T(8,128)(2,1)S(1)} %bitcast.26, bf16[32,32,128]{2,1,0:T(8,128)(2,1)S(1)} %bitcast.31, bf16[32,32,128]{2,1,0:T(8,128)(2,1)S(1)} %bitcast.35, ...), custom_call_target="tpu_custom_call" | custom-call | flops 67108864 | bytes 6291456 | tf_op jit(solution)/shard_map/old_sum/pallas_call | solution.py:79
  199.5 4.2 %all-to-all-start.5 = ((bf16[16,2,32,128]{3,2,1,0:T(8,128)(2,1)}), bf16[16,2,32,128]{3,2,1,0:T(8,128)(2,1)S(1)}, u32[]{:S(2)}, u32[]{:S(2)}) async-start(bf16[16,2,32,128]{3,2,1,0:T(8,128)(2,1)} %get-tuple-element.39), calls=%async_computation.5 | async-start | bytes 524288 | tf_op jit(solution)/shard_map/all_to_all | solution.py:229
  203.7 5.5 %old_sum.13.old_ref = f32[2,32,128]{2,1,0:T(8,128)S(1)} custom-call(s32[64]{0:T(128)S(1)} %squeeze.63.code_ref, bf16[544,32,128]{2,1,0:T(8,128)(2,1)} %constant_dynamic-update-slice_fusion.4.refs_0_, bf16[32,32,128]{2,1,0:T(8,128)(2,1)S(1)} %bitcast.27, bf16[32,32,128]{2,1,0:T(8,128)(2,1)S(1)} %bitcast.32, bf16[32,32,128]{2,1,0:T(8,128)(2,1)S(1)} %bitcast.36, ...), custom_call_target="tpu_custom_call" | custom-call | flops 67108864 | bytes 6291456 | tf_op jit(solution)/shard_map/old_sum/pallas_call | solution.py:79
  220.9 19.9 %collective-permute-start.40 = (bf16[7,32,128]{2,1,0:T(8,128)(2,1)S(1)}, bf16[7,32,128]{2,1,0:T(8,128)(2,1)S(1)}, u32[]{:S(2)}, u32[]{:S(2)}) collective-permute-start(bf16[7,32,128]{2,1,0:T(8,128)(2,1)S(1)} %get-tuple-element.60), channel_id=1, source_target_pairs={{0,4},{4,0},{1,5},{5,1},{2,6},{6,2},{3,7},{7,3},{8,12},{12,8},{9,1... | collective-permute-start | bytes 172040 | tf_op jit(solution)/shard_map/ppermute | solution.py:21
  (151 shorter events, 118.7 us)
Async XLA Ops:
  0.0 79.1 %collective-permute-start.16 = (bf16[7,1,32,128,128]{4,3,2,1,0:T(8,128)(2,1)}, bf16[7,1,32,128,128]{4,3,2,1,0:T(8,128)(2,1)}, u32[]{:S(2)}, u32[]{:S(2)}) collective-permute-start(bf16[7,1,32,128,128]{4,3,2,1,0:T(8,128)(2,1)} %own_ref.11), channel_id=1, source_target_pairs={{0,4},{4,0},{1,5},{5,1},{2,6},{6,2},{3,7},{7,3},{8,12},{12,8},{9,1... | collective-permute-start | bytes 22020104 | tf_op jit(solution)/shard_map/ppermute | solution.py:21
  5.8 10.1 %collective-permute-start.2 = (bf16[17,32,128]{2,1,0:T(8,128)(2,1)S(1)}, bf16[17,32,128]{2,1,0:T(8,128)(2,1)S(1)}, u32[]{:S(2)}, u32[]{:S(2)}) collective-permute-start(bf16[17,32,128]{2,1,0:T(8,128)(2,1)S(1)} %get-tuple-element.45), channel_id=1, source_target_pairs={{0,64},{32,96},{64,0},{96,32},{1,65},{33,97},{65,1},{97,33},{2,66}... | collective-permute-start | bytes 417800 | tf_op jit(solution)/shard_map/ppermute | solution.py:25
  9.1 9.4 %collective-permute-start.3 = (bf16[17,32,128]{2,1,0:T(8,128)(2,1)S(1)}, bf16[17,32,128]{2,1,0:T(8,128)(2,1)S(1)}, u32[]{:S(2)}, u32[]{:S(2)}) collective-permute-start(bf16[17,32,128]{2,1,0:T(8,128)(2,1)S(1)} %get-tuple-element.45), channel_id=1, source_target_pairs={{0,96},{32,64},{64,32},{96,0},{1,97},{33,65},{65,33},{97,1},{2,98}... | collective-permute-start | bytes 417800 | tf_op jit(solution)/shard_map/ppermute | solution.py:25
  18.6 14.7 %collective-permute-start.4 = (bf16[68,32,128]{2,1,0:T(8,128)(2,1)S(1)}, bf16[68,32,128]{2,1,0:T(8,128)(2,1)S(1)}, u32[]{:S(2)}, u32[]{:S(2)}) collective-permute-start(bf16[68,32,128]{2,1,0:T(8,128)(2,1)S(1)} %pad_maximum_fusion), channel_id=1, source_target_pairs={{0,8},{8,16},{16,24},{24,0},{1,9},{9,17},{17,25},{25,1},{2,10},{10... | collective-permute-start | bytes 1671176 | tf_op jit(solution)/shard_map/ppermute | solution.py:29
  19.9 15.4 %collective-permute-start.5 = (bf16[68,32,128]{2,1,0:T(8,128)(2,1)S(1)}, bf16[68,32,128]{2,1,0:T(8,128)(2,1)S(1)}, u32[]{:S(2)}, u32[]{:S(2)}) collective-permute-start(bf16[68,32,128]{2,1,0:T(8,128)(2,1)S(1)} %pad_maximum_fusion), channel_id=1, source_target_pairs={{0,24},{8,0},{16,8},{24,16},{1,25},{9,1},{17,9},{25,17},{2,26},{10... | collective-permute-start | bytes 1671176 | tf_op jit(solution)/shard_map/ppermute | solution.py:30
  21.5 65.6 %collective-permute-start.21 = (bf16[8,1,128,128]{3,2,1,0:T(8,128)(2,1)}, bf16[8,1,128,128]{3,2,1,0:T(8,128)(2,1)S(1)}, u32[]{:S(2)}, u32[]{:S(2)}) collective-permute-start(bf16[8,1,128,128]{3,2,1,0:T(8,128)(2,1)} %refs_6_.3), channel_id=1, source_target_pairs={{0,4},{4,0},{1,5},{5,1},{2,6},{6,2},{3,7},{7,3},{8,12},{12,8},{9,1... | collective-permute-start | bytes 786440 | tf_op jit(solution)/shard_map/ppermute | solution.py:21
  22.7 11.3 %collective-permute-start.8 = (bf16[17,32,128]{2,1,0:T(8,128)(2,1)S(1)}, bf16[17,32,128]{2,1,0:T(8,128)(2,1)S(1)}, u32[]{:S(2)}, u32[]{:S(2)}) collective-permute-start(bf16[17,32,128]{2,1,0:T(8,128)(2,1)S(1)} %get-tuple-element.46), channel_id=1, source_target_pairs={{0,4},{4,0},{1,5},{5,1},{2,6},{6,2},{3,7},{7,3},{8,12},{12,8},{9,1... | collective-permute-start | bytes 417800 | tf_op jit(solution)/shard_map/ppermute | solution.py:21
  33.3 7.7 %collective-permute-start.6 = (bf16[34,32,128]{2,1,0:T(8,128)(2,1)S(1)}, bf16[34,32,128]{2,1,0:T(8,128)(2,1)S(1)}, u32[]{:S(2)}, u32[]{:S(2)}) collective-permute-start(bf16[34,32,128]{2,1,0:T(8,128)(2,1)S(1)} %slice.146), channel_id=1, source_target_pairs={{0,8},{8,16},{16,24},{24,0},{1,9},{9,17},{17,25},{25,1},{2,10},{10... | collective-permute-start | bytes 835592 | tf_op jit(solution)/shard_map/ppermute | solution.py:32
  34.1 11.4 %collective-permute-start.9 = (bf16[17,32,128]{2,1,0:T(8,128)(2,1)S(1)}, bf16[17,32,128]{2,1,0:T(8,128)(2,1)S(1)}, u32[]{:S(2)}, u32[]{:S(2)}) collective-permute-start(bf16[17,32,128]{2,1,0:T(8,128)(2,1)S(1)} %collective-permute-done.8), channel_id=1, source_target_pairs={{0,8},{8,0},{16,24},{24,16},{1,9},{9,1},{17,25},{25,17},{2,10},{10... | collective-permute-start | bytes 417800 | tf_op jit(solution)/shard_map/ppermute | solution.py:25
  35.3 7.9 %collective-permute-start.7 = (bf16[34,32,128]{2,1,0:T(8,128)(2,1)S(1)}, bf16[34,32,128]{2,1,0:T(8,128)(2,1)S(1)}, u32[]{:S(2)}, u32[]{:S(2)}) collective-permute-start(bf16[34,32,128]{2,1,0:T(8,128)(2,1)S(1)} %slice.147), channel_id=1, source_target_pairs={{0,24},{8,0},{16,8},{24,16},{1,25},{9,1},{17,9},{25,17},{2,26},{10... | collective-permute-start | bytes 835592 | tf_op jit(solution)/shard_map/ppermute | solution.py:33
  41.1 6.3 %collective-permute-start.10 = (bf16[17,32,128]{2,1,0:T(8,128)(2,1)S(1)}, bf16[17,32,128]{2,1,0:T(8,128)(2,1)S(1)}, u32[]{:S(2)}, u32[]{:S(2)}) collective-permute-start(bf16[17,32,128]{2,1,0:T(8,128)(2,1)S(1)} %collective-permute-done.8), channel_id=1, source_target_pairs={{0,16},{8,24},{16,0},{24,8},{1,17},{9,25},{17,1},{25,9},{2,18},{10... | collective-permute-start | bytes 417800 | tf_op jit(solution)/shard_map/ppermute | solution.py:25
  43.2 7.1 %collective-permute-start.11 = (bf16[17,32,128]{2,1,0:T(8,128)(2,1)S(1)}, bf16[17,32,128]{2,1,0:T(8,128)(2,1)S(1)}, u32[]{:S(2)}, u32[]{:S(2)}) collective-permute-start(bf16[17,32,128]{2,1,0:T(8,128)(2,1)S(1)} %collective-permute-done.8), channel_id=1, source_target_pairs={{0,24},{8,16},{16,8},{24,0},{1,25},{9,17},{17,9},{25,1},{2,26},{10... | collective-permute-start | bytes 417800 | tf_op jit(solution)/shard_map/ppermute | solution.py:25
  51.0 11.8 %collective-permute-start.12 = (bf16[68,32,128]{2,1,0:T(8,128)(2,1)S(1)}, bf16[68,32,128]{2,1,0:T(8,128)(2,1)S(1)}, u32[]{:S(2)}, u32[]{:S(2)}) collective-permute-start(bf16[68,32,128]{2,1,0:T(8,128)(2,1)S(1)} %get-tuple-element.47), channel_id=1, source_target_pairs={{0,32},{32,64},{64,96},{96,0},{1,33},{33,65},{65,97},{97,1},{2,34}... | collective-permute-start | bytes 1671176 | tf_op jit(solution)/shard_map/ppermute | solution.py:29
  54.7 32.3 %collective-permute-start.20 = (bf16[8,1,32,128]{3,2,1,0:T(8,128)(2,1)S(1)}, bf16[8,1,32,128]{3,2,1,0:T(8,128)(2,1)S(1)}, u32[]{:S(2)}, u32[]{:S(2)}) collective-permute-start(bf16[8,1,32,128]{3,2,1,0:T(8,128)(2,1)S(1)} %get-tuple-element.56), channel_id=1, source_target_pairs={{0,4},{4,0},{1,5},{5,1},{2,6},{6,2},{3,7},{7,3},{8,12},{12,8},{9,1... | collective-permute-start | bytes 196616 | tf_op jit(solution)/shard_map/ppermute | solution.py:21
  55.5 14.6 %collective-permute-start.13 = (bf16[68,32,128]{2,1,0:T(8,128)(2,1)S(1)}, bf16[68,32,128]{2,1,0:T(8,128)(2,1)S(1)}, u32[]{:S(2)}, u32[]{:S(2)}) collective-permute-start(bf16[68,32,128]{2,1,0:T(8,128)(2,1)S(1)} %get-tuple-element.47), channel_id=1, source_target_pairs={{0,96},{32,0},{64,32},{96,64},{1,97},{33,1},{65,33},{97,65},{2,98}... | collective-permute-start | bytes 1671176 | tf_op jit(solution)/shard_map/ppermute | solution.py:30
  62.8 12.5 %collective-permute-start.14 = (bf16[34,32,128]{2,1,0:T(8,128)(2,1)S(1)}, bf16[34,32,128]{2,1,0:T(8,128)(2,1)S(1)}, u32[]{:S(2)}, u32[]{:S(2)}) collective-permute-start(bf16[34,32,128]{2,1,0:T(8,128)(2,1)S(1)} %slice.148), channel_id=1, source_target_pairs={{0,32},{32,64},{64,96},{96,0},{1,33},{33,65},{65,97},{97,1},{2,34}... | collective-permute-start | bytes 835592 | tf_op jit(solution)/shard_map/ppermute | solution.py:32
  70.1 8.3 %collective-permute-start.15 = (bf16[34,32,128]{2,1,0:T(8,128)(2,1)S(1)}, bf16[34,32,128]{2,1,0:T(8,128)(2,1)S(1)}, u32[]{:S(2)}, u32[]{:S(2)}) collective-permute-start(bf16[34,32,128]{2,1,0:T(8,128)(2,1)S(1)} %slice.149), channel_id=1, source_target_pairs={{0,96},{32,0},{64,32},{96,64},{1,97},{33,1},{65,33},{97,65},{2,98}... | collective-permute-start | bytes 835592 | tf_op jit(solution)/shard_map/ppermute | solution.py:33
  91.3 13.8 %all-to-all-start = ((bf16[16,2,32,128]{3,2,1,0:T(8,128)(2,1)}), bf16[16,2,32,128]{3,2,1,0:T(8,128)(2,1)S(1)}, u32[]{:S(2)}, u32[]{:S(2)}) async-start(bf16[16,2,32,128]{3,2,1,0:T(8,128)(2,1)} %get-tuple-element.24), calls=%async_computation | async-start | bytes 524288 | tf_op jit(solution)/shard_map/all_to_all | solution.py:229
  113.9 11.0 %all-to-all-start.1 = ((bf16[16,2,32,128]{3,2,1,0:T(8,128)(2,1)}), bf16[16,2,32,128]{3,2,1,0:T(8,128)(2,1)S(1)}, u32[]{:S(2)}, u32[]{:S(2)}) async-start(bf16[16,2,32,128]{3,2,1,0:T(8,128)(2,1)} %get-tuple-element.27), calls=%async_computation.1 | async-start | bytes 524288 | tf_op jit(solution)/shard_map/all_to_all | solution.py:229
  136.2 11.0 %all-to-all-start.2 = ((bf16[16,2,32,128]{3,2,1,0:T(8,128)(2,1)}), bf16[16,2,32,128]{3,2,1,0:T(8,128)(2,1)S(1)}, u32[]{:S(2)}, u32[]{:S(2)}) async-start(bf16[16,2,32,128]{3,2,1,0:T(8,128)(2,1)} %get-tuple-element.30), calls=%async_computation.2 | async-start | bytes 524288 | tf_op jit(solution)/shard_map/all_to_all | solution.py:229
  156.4 11.4 %all-to-all-start.3 = ((bf16[16,2,32,128]{3,2,1,0:T(8,128)(2,1)}), bf16[16,2,32,128]{3,2,1,0:T(8,128)(2,1)S(1)}, u32[]{:S(2)}, u32[]{:S(2)}) async-start(bf16[16,2,32,128]{3,2,1,0:T(8,128)(2,1)} %get-tuple-element.33), calls=%async_computation.3 | async-start | bytes 524288 | tf_op jit(solution)/shard_map/all_to_all | solution.py:229
  178.5 11.4 %all-to-all-start.4 = ((bf16[16,2,32,128]{3,2,1,0:T(8,128)(2,1)}), bf16[16,2,32,128]{3,2,1,0:T(8,128)(2,1)S(1)}, u32[]{:S(2)}, u32[]{:S(2)}) async-start(bf16[16,2,32,128]{3,2,1,0:T(8,128)(2,1)} %get-tuple-element.36), calls=%async_computation.4 | async-start | bytes 524288 | tf_op jit(solution)/shard_map/all_to_all | solution.py:229
  199.5 11.8 %all-to-all-start.5 = ((bf16[16,2,32,128]{3,2,1,0:T(8,128)(2,1)}), bf16[16,2,32,128]{3,2,1,0:T(8,128)(2,1)S(1)}, u32[]{:S(2)}, u32[]{:S(2)}) async-start(bf16[16,2,32,128]{3,2,1,0:T(8,128)(2,1)} %get-tuple-element.39), calls=%async_computation.5 | async-start | bytes 524288 | tf_op jit(solution)/shard_map/all_to_all | solution.py:229
  220.9 20.8 %collective-permute-start.40 = (bf16[7,32,128]{2,1,0:T(8,128)(2,1)S(1)}, bf16[7,32,128]{2,1,0:T(8,128)(2,1)S(1)}, u32[]{:S(2)}, u32[]{:S(2)}) collective-permute-start(bf16[7,32,128]{2,1,0:T(8,128)(2,1)S(1)} %get-tuple-element.60), channel_id=1, source_target_pairs={{0,4},{4,0},{1,5},{5,1},{2,6},{6,2},{3,7},{7,3},{8,12},{12,8},{9,1... | collective-permute-start | bytes 172040 | tf_op jit(solution)/shard_map/ppermute | solution.py:21
  (27 other events, 265.7 us)

commit v2 on v0

v2 whole, which is shorter than its diff:
```python
import functools

import jax
import jax.numpy as jnp
from jax import lax
from jax.experimental import pallas as pl
from jax.experimental.pallas import tpu as pltpu
from jax.sharding import Mesh, PartitionSpec as P

ROWS = ("z", "y", "core")
VMEM_LIMIT = 48 * 1024 * 1024


def xor_pairs(n, k):
    return [(i, i ^ k) for i in range(n)]


def shift_pairs(n, k):
    return [(i, (i + k) % n) for i in range(n)]


def swap_cores(v):
    return lax.ppermute(v, "core", xor_pairs(2, 1))


def direct_gather(v, axis):
    return jnp.concatenate([v] + [lax.ppermute(v, axis, xor_pairs(4, k)) for k in (1, 2, 3)])


def ring_gather(v, axis):
    before = lax.ppermute(v, axis, shift_pairs(4, 1))
    after = lax.ppermute(v, axis, shift_pairs(4, 3))
    half = v.shape[0] // 2
    far_a = lax.ppermute(before[:half], axis, shift_pairs(4, 1))
    far_b = lax.ppermute(after[half:], axis, shift_pairs(4, 3))
    return [v, before, after, far_a, far_b]


def nt_dot(x, a):
    return lax.dot_general(x, a, (((1,), (1,)), ((), ())), preferred_element_type=jnp.float32)


GROUP = 8
UNROLL = 4
CAPACITY = (12, 14, 16, 18, 19, 20)
FRESH_CAPACITY = 24
MIDDLE_CAPACITY = 52
CHUNKS = ((2, 3), (4, 5), (6,), (7,))


def chunk_of(level):
    for n, chunk in enumerate(CHUNKS):
        if level in chunk:
            before = sum(CAPACITY[one - 2] for one in chunk if one < level)
            return n, before, sum(CAPACITY[one - 2] for one in chunk)


def call(kernel, name, operands, in_spaces, outs, out_spaces, scratch, flops=0, bytes_accessed=0):
    return pl.pallas_call(
        kernel,
        out_shape=outs,
        in_specs=[pl.BlockSpec(memory_space=space) for space in in_spaces],
        out_specs=[pl.BlockSpec(memory_space=space) for space in out_spaces],
        scratch_shapes=scratch,
        compiler_params=pltpu.CompilerParams(vmem_limit_bytes=VMEM_LIMIT),
        cost_estimate=pl.CostEstimate(flops=flops, bytes_accessed=bytes_accessed, transcendentals=0),
        name=name,
    )(*operands)


def gather_sum(level, code_ref, picks, own_ref, other_ref, out_ref, blocks, block_sems):
    slots = code_ref.shape[1]
    per_row = slots // 2
    loads = [
        pltpu.make_async_copy(a_ref.at[level - 1, 0], blocks.at[pl.ds(r * per_row, per_row)], block_sems.at[r])
        for r, a_ref in enumerate((own_ref, other_ref))
    ]
    for r in range(2):
        loads[r].wait()
        total = None
        for g in range(r * per_row, (r + 1) * per_row, GROUP):
            xs, group = [], []
            for k in range(g, g + GROUP):
                code = code_ref[level - 1, k]
                kept = (code >= 0).astype(jnp.float32)
                xs.append((picks(k, jnp.maximum(code, 0)).astype(jnp.float32) * kept).astype(jnp.bfloat16))
                group.append(blocks[k])
            part = nt_dot(jnp.concatenate(xs, axis=1), jnp.concatenate(group, axis=1))
            total = part if total is None else total + part
        out_ref[r] = total


def start_blocks(levels, own_ref, other_ref, blocks, block_sems):
    per_row = blocks.shape[1] // 2
    for n, level in enumerate(levels):
        for r, a_ref in enumerate((own_ref, other_ref)):
            target = blocks.at[n, pl.ds(r * per_row, per_row)]
            pltpu.make_async_copy(a_ref.at[level - 1, 0], target, block_sems.at[n, r]).start()


def first_kernel(levels, code_ref, flag_ref, *refs):
    sources, refs = refs[:-9], refs[-9:]
    own_ref, other_ref, out_ref, store_ref, blocks, block_sems, pack_sems, packed, store_sem = refs
    start_blocks(levels, own_ref, other_ref, blocks, block_sems)
    packs, start = [], 0
    for i, source in enumerate(sources):
        packs.append(pltpu.make_async_copy(source, packed.at[pl.ds(start, source.shape[0])], pack_sems.at[i]))
        start += source.shape[0]
    for pack in packs:
        pack.start()
    for pack in packs:
        pack.wait()
    keep = pltpu.make_async_copy(packed, store_ref.at[pl.ds(0, start)], store_sem)
    keep.start()
    for n, level in enumerate(levels):
        gather_sum(
            level, code_ref, lambda k, code: packed[code], own_ref, other_ref, out_ref.at[n], blocks.at[n], block_sems.at[n]
        )
    out_ref[0] = out_ref[0] + jnp.where(flag_ref[0] > 0, jnp.float32(jnp.nan), jnp.float32(0.0))
    keep.wait()


def known_kernel(levels, code_ref, store_ref, own_ref, other_ref, out_ref, blocks, block_sems, picked, pick_sem):
    slots = code_ref.shape[1]
    start_blocks(levels, own_ref, other_ref, blocks, block_sems)
    for n, level in enumerate(levels):

        def fetch(k, carry, n=n, level=level):
            place = jnp.maximum(code_ref[level - 1, k], 0)
            pltpu.make_async_copy(store_ref.at[place], picked.at[n * slots + k], pick_sem).start()
            return carry

        lax.fori_loop(0, slots, fetch, 0)
    pltpu.make_async_copy(store_ref.at[pl.ds(0, slots * len(levels))], picked, pick_sem).wait()
    for n, level in enumerate(levels):
        picks = lambda k, code, n=n: picked[n * slots + k]
        gather_sum(level, code_ref, picks, own_ref, other_ref, out_ref.at[n], blocks.at[n], block_sems.at[n])


def known_sums(levels, code, flag, sources, own, other):
    slots, one, some = code.shape[1], sources[0].shape[1:], len(levels)
    sums = jax.ShapeDtypeStruct((some, 2) + one, jnp.float32)
    scratch = [pltpu.VMEM((some, slots, one[1], one[1]), jnp.bfloat16), pltpu.SemaphoreType.DMA((some, 2))]
    cost = dict(
        flops=2 * some * slots * one[0] * one[1] * one[1], bytes_accessed=some * slots * one[1] * (one[1] + 2 * one[0]) * 4
    )
    spaces = [pl.ANY] * len(sources) + [pltpu.HBM] * 2
    if flag is None:
        scratch += [pltpu.VMEM((some * slots,) + one, jnp.bfloat16), pltpu.SemaphoreType.DMA]
        kernel = functools.partial(known_kernel, levels)
        operands = (code, *sources, own, other)
        return call(kernel, "known_sums", operands, [pltpu.SMEM] + spaces, [sums], [pltpu.VMEM], scratch, **cost)[0]
    known = sum(v.shape[0] for v in sources)
    scratch += [
        pltpu.SemaphoreType.DMA((len(sources),)),
        pltpu.VMEM((known,) + one, jnp.bfloat16),
        pltpu.SemaphoreType.DMA,
    ]
    store = jax.ShapeDtypeStruct((2048,) + one, jnp.bfloat16)
    kernel = functools.partial(first_kernel, levels)
    operands = (code, flag, *sources, own, other)
    spaces = [pltpu.SMEM] * 2 + spaces
    return call(kernel, "first_sums", operands, spaces, [sums, store], [pltpu.VMEM, pltpu.HBM], scratch, **cost)


def near_kernel(rank_ref, off_ref, *refs):
    outs, (blocks, sem, out_sems) = refs[: len(CHUNKS)], refs[len(CHUNKS) :]
    slots = rank_ref.shape[1]
    places = []
    for level in range(2, 2 + len(CAPACITY)):
        n, before, _ = chunk_of(level)
        places.append(sum(sum(CAPACITY[one - 2] for one in chunk) for chunk in CHUNKS[:n]) + before)
        if before == 0:
            blocks[places[-1]] = jnp.zeros(blocks.shape[1:], blocks.dtype)

    for level, place in zip(range(2, 2 + len(CAPACITY)), places):

        def copy_of(k, level=level, place=place):
            target = place + rank_ref[level - 1, k]
            return pltpu.make_async_copy(off_ref.at[level - 1, 0, k], blocks.at[target], sem.at[target])

        def load(k, carry, level=level, copy_of=copy_of):
            @pl.when(rank_ref[level - 1, k] >= 0)
            def _():
                copy_of(k).start()

            return carry

        lax.fori_loop(0, slots, load, 0)

    for level, place in zip(range(2, 2 + len(CAPACITY)), places):

        def wait(k, carry, level=level, place=place):
            @pl.when(rank_ref[level - 1, k] >= 0)
            def _():
                target = place + rank_ref[level - 1, k]
                pltpu.make_async_copy(off_ref.at[level - 1, 0, k], blocks.at[target], sem.at[target]).wait()

            return carry

        lax.fori_loop(0, slots, wait, 0)
    start, stores = 0, []
    for n, out in enumerate(outs):
        stores.append(pltpu.make_async_copy(blocks.at[pl.ds(start, out.shape[0])], out, out_sems.at[n]))
        stores[-1].start()
        start += out.shape[0]
    for store in stores:
        store.wait()


def near_blocks(rank, off):
    block = off.shape[-1]
    sizes = [sum(CAPACITY[one - 2] for one in chunk) for chunk in CHUNKS]
    outs = [jax.ShapeDtypeStruct((size, block, block), jnp.bfloat16) for size in sizes]
    scratch = [
        pltpu.VMEM((sum(sizes), block, block), jnp.bfloat16),
        pltpu.SemaphoreType.DMA((sum(sizes),)),
        pltpu.SemaphoreType.DMA((len(sizes),)),
    ]
    return call(
        near_kernel, "near_blocks", (rank, off), [pltpu.SMEM, pltpu.HBM], outs, [pltpu.HBM] * len(sizes), scratch
    )


def add_listed(total, count, entry_of, block_of, solved_of, ready=None):
    def step(j, total):
        xs, blocks = [], []
        for t in range(UNROLL):
            i = j * UNROLL + t
            entry = entry_of(i)
            if ready is not None:
                ready(i)
            kept = ((entry >> 8) & 1).astype(jnp.float32)
            xs.append((solved_of(entry & 255).astype(jnp.float32) * kept).astype(jnp.bfloat16))
            blocks.append(block_of(i))
        return total + nt_dot(jnp.concatenate(xs, axis=1), jnp.concatenate(blocks, axis=1))

    return lax.fori_loop(0, (count + UNROLL - 1) // UNROLL, step, total)


def middle_kernel(level, counts_ref, fresh_ref, middle_ref, *refs):
    solved, refs = refs[: level - 2], refs[level - 2 :]
    own_ref, other_ref, out_ref, near_ref, blocks, sems, near_sems = refs[:7]
    fresh_max, middle_max = fresh_ref.shape[1], middle_ref.shape[1]
    at = 2 * (level - 1)
    rounded = lambda n: (n + UNROLL - 1) // UNROLL * UNROLL

    def copies(r, source):
        fresh = lambda i: pltpu.make_async_copy(
            source.at[fresh_ref[at + r, i] >> 9], near_ref.at[r * fresh_max + i], near_sems.at[r * fresh_max + i]
        )
        middle = lambda i: pltpu.make_async_copy(
            source.at[middle_ref[at + r, i] >> 9], blocks.at[r * middle_max + i], sems.at[r * middle_max + i]
        )
        return fresh, middle

    def each(count, do):
        def body(i, carry):
            do(i)
            return carry

        lax.fori_loop(0, rounded(count), body, 0)

    for r, source in enumerate((own_ref, other_ref)):
        fresh, middle = copies(r, source)
        if solved:
            each(counts_ref[1, at + r], lambda i: middle(i).start())
        each(counts_ref[0, at + r], lambda i: fresh(i).start())
    if solved:
        solved_ref = refs[7]
        for i, one in enumerate(solved):
            solved_ref[i * one.shape[0] : (i + 1) * one.shape[0]] = one[...]
    for r, source in enumerate((own_ref, other_ref)):
        _, middle = copies(r, source)
        total = jnp.zeros(out_ref.shape[1:], jnp.float32)
        if solved:
            total = add_listed(
                total,
                counts_ref[1, at + r],
                lambda i: middle_ref[at + r, i],
                lambda i: blocks[r * middle_max + i],
                lambda place: solved_ref[place],
                lambda i: middle(i).wait(),
            )
        out_ref[r] = total
    for r, source in enumerate((own_ref, other_ref)):
        fresh, _ = copies(r, source)
        each(counts_ref[0, at + r], lambda i: fresh(i).wait())


def middle_sum(level, counts, fresh, middle, solved, own, other, rhs_cols):
    block = own.shape[-1]
    one = (rhs_cols, block)
    outs = [
        jax.ShapeDtypeStruct((2,) + one, jnp.float32),
        jax.ShapeDtypeStruct((2 * fresh.shape[1], block, block), jnp.bfloat16),
    ]
    scratch = [
        pltpu.VMEM((2 * middle.shape[1], block, block), jnp.bfloat16),
        pltpu.SemaphoreType.DMA((2 * middle.shape[1],)),
        pltpu.SemaphoreType.DMA((2 * fresh.shape[1],)),
    ]
    if solved:
        scratch.append(pltpu.VMEM((sum(v.shape[0] for v in solved),) + one, jnp.bfloat16))
    spaces = [pltpu.SMEM] * 3 + [pltpu.VMEM] * len(solved) + [pltpu.HBM] * 2
    operands = (counts, fresh, middle, *solved, own, other)
    kernel = functools.partial(middle_kernel, level)
    return call(
        kernel, "middle_sum", operands, spaces, outs, [pltpu.VMEM] * 2, scratch, 2 * 40 * rhs_cols * block**2, 8 << 20
    )


def solve_kernel(level, at, last, *refs):
    near = level > 1
    if near:
        (counts_ref, fresh_ref, middle_ref, near_ref, solved_ref), refs = refs[:5], refs[5:]
    p0, p1, p2, p3, rhs_ref, own_d_ref, other_d_ref, out_ref = refs[:8]
    for r, d_ref in enumerate((own_d_ref, other_d_ref)):
        coupled = (p0[at, r] + p1[at, r]) + (p2[at, r] + p3[at, r])
        if near:
            row = 2 * (level - 1) + r
            first = level - 2
            place = first * 32
            fresh_max = fresh_ref.shape[1]
            coupled = add_listed(
                coupled + middle_ref[r],
                counts_ref[0, row],
                lambda i: fresh_ref[row, i],
                lambda i: near_ref[r * fresh_max + i],
                lambda code: solved_ref[jnp.maximum(code - place, 0)],
            )
        reduced = (rhs_ref[level, r].astype(jnp.float32) - coupled).astype(jnp.bfloat16)
        solved = nt_dot(reduced, d_ref[level, 0]).astype(jnp.bfloat16)
        out_ref[r] = solved
        if not last:
            refs[9][lax.axis_index("core") ^ r] = solved
    if not last:
        all_ref, both, sems = refs[8:]
        sends = [pltpu.make_async_copy(both, all_ref.at[i], sems.at[i]) for i in range(all_ref.shape[0])]
        for send in sends:
            send.start()
        for send in sends:
            send.wait()


def solve_level(level, at, near, partials, rhs, own_d, other_d, copies):
    one = partials[0].shape[2:]
    outs, spaces, scratch = [jax.ShapeDtypeStruct((2,) + one, jnp.bfloat16)], [pltpu.VMEM], []
    if copies:
        outs.append(jax.ShapeDtypeStruct((copies, 2) + one, jnp.bfloat16))
        spaces.append(pltpu.HBM)
        scratch = [pltpu.VMEM((2,) + one, jnp.bfloat16), pltpu.SemaphoreType.DMA((copies,))]
    in_spaces = ([pltpu.SMEM] * 2 + [pltpu.VMEM] * 3 if near else []) + [pltpu.VMEM] * 7
    kernel = functools.partial(solve_kernel, level, at, not copies)
    return call(
        kernel, "solve_level", (*near, *partials, rhs, own_d, other_d), in_spaces, outs, spaces, scratch
    )


def plain(rhs, boundary, diag_inv, off_blocks, coupling, present):
    levels, _, rhs_cols, block = rhs.shape
    outer_all = lax.all_gather(boundary, ROWS, axis=0, tiled=True)
    outer, width = outer_all.shape[0], 32
    empty = jnp.zeros((levels * width, rhs_cols, block), jnp.bfloat16)
    solved = jnp.concatenate([outer_all, empty], axis=0)
    results = []
    for level in range(levels):
        target = rhs[level, 0].astype(jnp.float32)
        if level > 0:
            picked = jnp.take(solved, coupling[level - 1, 0], axis=0)
            picked = picked * present[level - 1, 0].astype(jnp.bfloat16)[:, None, None]
            partial_value = jnp.einsum(
                "kab,krb->ra", off_blocks[level - 1, 0], picked, preferred_element_type=jnp.float32
            )
            target = target - lax.psum(partial_value, "x")
        own = jnp.einsum(
            "rb,ab->ra", target.astype(jnp.bfloat16), diag_inv[level, 0], preferred_element_type=jnp.float32
        ).astype(jnp.bfloat16)
        fresh = lax.all_gather(own[None], ROWS, axis=0, tiled=True)
        solved = solved.at[outer + level * width : outer + (level + 1) * width].set(fresh)
        results.append(own)
    return jnp.stack(results)[:, None]


def tied(value, to):
    return lax.optimization_barrier((value, to))


def on_device(rhs, boundary, diag_inv, off_blocks, coupling, present):
    levels, _, rhs_cols, block = rhs.shape
    outer_each = boundary.shape[0]
    outer = outer_each * 32
    half = rhs_cols // 2
    z, y, core, x = (lax.axis_index(a) for a in ("z", "y", "core", "x"))

    def my_half(v, axis):
        return lax.dynamic_slice_in_dim(v, core * half, half, axis)

    def their_half(v, axis):
        return lax.dynamic_slice_in_dim(v, (1 - core) * half, half, axis)

    first = jnp.einsum("rb,ab->ra", rhs[0, 0], diag_inv[0, 0], preferred_element_type=jnp.float32).astype(jnp.bfloat16)
    known = jnp.concatenate([boundary, first[None]])
    known_own, known_other = tied(my_half(known, 1), swap_cores(their_half(known, 1)))

    code_own = (coupling + 1024 * present)[:, 0]
    inside = lambda code: (code >= 1024 + outer + 32) & (jnp.arange(levels - 1) > 0)[:, None]
    own_inside = inside(code_own)
    limits = jnp.array((0,) + CAPACITY, jnp.int32)[:, None]
    own_rank = jnp.cumsum(own_inside.astype(jnp.int32), axis=1) - 1
    own_rank = jnp.where(own_inside & (own_rank < limits), own_rank, -1)
    nears = near_blocks(own_rank, off_blocks)
    near_own = [lax.all_gather(v, "x", axis=0, tiled=True) for v in nears]
    near_other = [swap_cores(v) for v in near_own]

    code_both = jnp.stack([code_own, swap_cores(code_own)], axis=1)
    rhs_both = jnp.concatenate([my_half(rhs, 2), swap_cores(their_half(rhs, 2))], axis=1)
    diag_other = swap_cores(diag_inv)
    off_sent, known_own = tied(off_blocks, known_own)
    off_other = swap_cores(off_sent)

    color_a = ring_gather(direct_gather(known_own, "z"), "y")
    color_b = ring_gather(direct_gather(known_other, "y"), "z")

    keep, index = code_both >= 1024, code_both % 1024
    in_outer = index < outer
    row = jnp.where(in_outer, index // outer_each, index - outer)
    member = jnp.where(in_outer, index % outer_each, outer_each)
    src_z, src_y, src_core = row // 8, (row // 2) % 4, row % 2
    each = outer_each + 1
    mine_too = src_core == core
    away = jnp.where(mine_too, src_y - y, src_z - z) % 4
    place = jnp.where(mine_too, src_z ^ z, src_y ^ y) * each + member
    slot_of = jnp.where(away == 3, 1, jnp.where(away == 1, 2, jnp.where(away == 2, 3, 0)))
    known_place = jnp.where(mine_too, 0, 16 * each) + slot_of * (4 * each) + place
    known_code = jnp.where(keep & (index < outer + 32), known_place, -1).reshape(levels - 1, -1)

    every = jnp.stack([code_both] + [lax.ppermute(code_both, "x", xor_pairs(4, k)) for k in (1, 2, 3)], axis=2)
    this = jnp.arange(levels - 1)[:, None, None, None]
    every_inside = (every >= 1024 + outer + 32) & (this > 0)
    rank = jnp.cumsum(every_inside.astype(jnp.int32), axis=3) - 1
    solved_place = every - (1024 + outer + 32)
    at_x = (x ^ jnp.arange(4))[:, None]
    chunk_size = jnp.array([0] + [chunk_of(level)[2] for level in range(2, levels)], jnp.int32)[:, None, None, None]
    chunk_start = jnp.array([0] + [chunk_of(level)[1] for level in range(2, levels)], jnp.int32)[:, None, None, None]
    entry = (at_x * chunk_size + chunk_start + rank) * 512 + 256 + solved_place
    is_fresh = every_inside & (solved_place >= (this - 1) * 32)
    is_middle = every_inside & ~is_fresh

    def listed(chosen, capacity):
        entries = jnp.where(chosen, entry, 0).reshape(2 * (levels - 1), -1)
        return -lax.sort(-entries, dimension=1)[:, :capacity], jnp.sum(chosen, axis=(2, 3), dtype=jnp.int32).reshape(-1)

    fresh_list, fresh_count = listed(is_fresh, FRESH_CAPACITY)
    middle_list, middle_count = listed(is_middle, MIDDLE_CAPACITY)
    inside_count = jnp.sum(every_inside, axis=3, dtype=jnp.int32)
    over = jnp.any(inside_count > limits[:, :, None]) | jnp.any(fresh_count > FRESH_CAPACITY)
    over = over | jnp.any(middle_count > MIDDLE_CAPACITY)
    flag = over.astype(jnp.int32).reshape(1)
    counts = jnp.stack([jnp.minimum(fresh_count, FRESH_CAPACITY), jnp.minimum(middle_count, MIDDLE_CAPACITY)])
    in_reach = lambda entries: jnp.minimum(entries, (4 * jnp.repeat(chunk_size.reshape(-1), 2)[:, None] - 1) * 512 + 511)
    fresh_list, middle_list = in_reach(fresh_list), in_reach(middle_list)
    fresh_list, middle_list = jnp.maximum(fresh_list, 0), jnp.maximum(middle_list, 0)

    def over_x(value):
        return [value] + [lax.ppermute(value, "x", xor_pairs(4, k)) for k in (1, 2, 3)]

    batches = ((1, 2), (3, 4), (5, 6), (7,))
    value, store = known_sums(batches[0], known_code, flag, color_a + color_b, off_blocks, off_other)
    sums = {level: (over_x_value, n) for over_x_value in [over_x(value)] for n, level in enumerate(batches[0])}
    own_rows, other_rows, solved_levels, pending = [], [], [], None
    near = ()
    for level in range(1, levels):
        last = level == levels - 1
        partials, at = sums[level]
        outs = solve_level(level, at, near, partials, rhs_both, diag_inv, diag_other, 0 if last else 16)
        own_rows.append(outs[0][0])
        other_rows.append(outs[0][1])
        if last:
            break
        tie, sent = tied(counts, outs[1])
        solved = lax.all_to_all(sent, ("z", "y"), 0, 0).reshape(32, half, block)
        if pending is not None:
            batch, value = pending
            value, _ = tied(value, sent)
            spread = over_x(value)
            sums.update({one: (spread, n) for n, one in enumerate(batch)})
            pending = None
        if level < len(batches):
            code, _ = tied(known_code, sent)
            pending = (batches[level], known_sums(batches[level], code, None, [store], off_blocks, off_other))
        n = chunk_of(level + 1)[0]
        middle, near_now = middle_sum(
            level + 1, tie, fresh_list, middle_list, solved_levels, near_own[n], near_other[n], half
        )
        near = (counts, fresh_list, middle, near_now, solved)
        solved_levels = solved_levels + [solved]

    given_up = jnp.any(solved_levels[0] != solved_levels[0])
    mine = jnp.stack(own_rows)
    theirs = swap_cores(jnp.stack(other_rows))
    low = jnp.where(core == 0, mine, theirs)
    high = jnp.where(core == 0, theirs, mine)
    rest = jnp.concatenate([low, high], axis=1)
    fast = jnp.concatenate([first[None], rest])[:, None]
    arguments = (rhs, boundary, diag_inv, off_blocks, coupling, present)
    return lax.cond(given_up, lambda fast, *arguments: plain(*arguments), lambda fast, *arguments: fast, fast, *arguments)


def solution(mesh):
    split = Mesh(mesh.devices.reshape(4, 4, 2, 4), ("z", "y", "core", "x"))
    in_specs = (
        P(None, ROWS, None, None),
        P(ROWS, None, None),
        P(None, ROWS, None, None),
        P(None, ROWS, "x", None, None),
        P(None, ROWS, "x"),
        P(None, ROWS, "x"),
    )
    return jax.shard_map(
        on_device, mesh=split, in_specs=in_specs, out_specs=P(None, ROWS, None, None), check_vma=False
    )
```

time: 390 us -> 371 us (0.951)
  blocking collectives: 274 us -> 0 us
  starting transfers between devices: 0.01 us -> 96.7 us
  waiting for transfers between devices: 29.9 us -> 126 us
  Pallas kernels: 0 us -> 89.2 us
  local copies, waits for them, and re-layouts: 53.1 us -> 22.3 us
  matrix products: 14.8 us -> 0.88 us
  other arithmetic: 1.5 us -> 14 us
  between operations: 13.7 us -> 17.9 us
    all_gather x7 -> x0, blocking collectives: 189 us -> none  [on_device(): fresh = lax.all_gather(own, 'row', axis=0, tiled=True)]
    pallas_call x0 -> x18, Pallas kernels: none -> 89.2 us  [call(): pl.pallas_call(kernel, out_shape=outs, in_specs=[pl.BlockSpec(memory_spac...]
    psum x7 -> x0, blocking collectives: 84.6 us -> none  [on_device(): target = target - lax.psum(partial_value, 'col')]
    ppermute x0 -> x39, starting transfers between devices: none -> 59.7 us  [the longest x10 18 us: swap_cores(): return lax.ppermute(v, 'core', xor_pairs(2, 1))]
    all_gather x1 -> x4, waiting for transfers between devices: 29.2 us -> 78.2 us  [on_device(): near_own = [lax.all_gather(v, 'x', axis=0, tiled=True) for v in nears]]
    ppermute x0 -> x39, waiting for transfers between devices: none -> 42.5 us  [the longest x2 14.4 us: ring_gather(): before = lax.ppermute(v, axis, shift_pairs(4, 1))]
    all_to_all x0 -> x6, starting transfers between devices: none -> 36.8 us  [on_device(): solved = lax.all_to_all(sent, ('z', 'y'), 0, 0).reshape(32, half, block)]
    gather x7 -> x0, local copies, waits for them, and re-layouts: 36.6 us -> none  [on_device(): jnp.take(solved, index.reshape(-1), axis=0)]
  transfers between devices with their start and end apart: 1 -> 49, of which waited for: 1 -> 18; matrix products, arithmetic and copies ran while one was open for 1% -> 5% of each run, Pallas kernels for 0% -> 18%
where the time goes in v2:
time: 371 us; the launch traced here: 367 us
  waiting for transfers between devices  126 us (34%)
  starting transfers between devices  96.7 us (26%)
  Pallas kernels  89.2 us (24%)
  local copies, waits for them, and re-layouts  22.3 us (6%)
  between operations  17.9 us (5%)
  other arithmetic  14 us (4%)
    pallas_call x18, Pallas kernels, call(): pl.pallas_call(kernel, out_shape=outs, in_specs=[pl.BlockSpec(memory_spac...  89.2 us
    all_gather x4, waiting for transfers between devices, on_device(): near_own = [lax.all_gather(v, 'x', axis=0, tiled=True) for v in nears]  78.2 us
    all_to_all x6, starting transfers between devices, on_device(): solved = lax.all_to_all(sent, ('z', 'y'), 0, 0).reshape(32, half, block)  36.8 us
    ppermute x10, starting transfers between devices, swap_cores(): return lax.ppermute(v, 'core', xor_pairs(2, 1))  18 us
    unnamed x70, local copies, waits for them, and re-layouts  17.5 us
    ppermute x2, waiting for transfers between devices, ring_gather(): before = lax.ppermute(v, axis, shift_pairs(4, 1))  14.4 us
    ppermute x12, starting transfers between devices, over_x(): lax.ppermute(value, 'x', xor_pairs(4, k))  13.4 us
    ppermute x6, starting transfers between devices, direct_gather(): lax.ppermute(v, axis, xor_pairs(4, k))  12.2 us
  transfers between devices with their start and end apart: 49, of which 18 were waited for; matrix products, arithmetic and copies ran while one was open for 5% of the time, Pallas kernels for 18%

profile of v2, /device:TPU:1, one launch (start us, length us, event | category | flops | bytes accessed | tf_op | source)
XLA Modules:
  0.0 367.1 jit_solution(6958668404080311114)
XLA Ops:
  9.3 9.2 %near_blocks.1 = (bf16[26,128,128]{2,1,0:T(8,128)(2,1)}, bf16[34,128,128]{2,1,0:T(8,128)(2,1)}, bf16[19,128,128]{2,1,0:T(8,128)(2,1)}, bf16[20,128,128]{2,1,0:T(8,128)(2,1)}) custom-call(s32[7,32]{1,0:T(8,128)S(1)} %and_select_fusion.rank_ref, bf16[7,1,32,128,128]{4,3,2,1,0:T(8,128)(2,1)} %own_ref.5), custom_call_target="tpu_custom_call" | custom-call | tf_op jit(solution)/shard_map/near_blocks/pallas_call | solution.py:59
  24.2 5.6 %collective-permute-done = s32[7,32]{1,0:T(8,128)S(1)} collective-permute-done((s32[7,32]{1,0:T(8,128)S(1)}, s32[7,32]{1,0:T(8,128)S(1)}, u32[]{:S(2)}, u32[]{:S(2)}) %collective-permute-start) | collective-permute-done | bytes 928 | tf_op jit(solution)/shard_map/ppermute | solution.py:23
  32.4 39.8 %all-gather.17.cloned.1.call-done.refs_2_.refs_3_ = bf16[136,128,128]{2,1,0:T(8,128)(2,1)} async-done(((bf16[34,128,128]{2,1,0:T(8,128)(2,1)}), bf16[136,128,128]{2,1,0:T(8,128)(2,1)}) %all-gather.17.cloned.1.call-update) | async-done | bytes 4456464 | tf_op jit(solution)/shard_map/all_gather | solution.py:413
  85.6 30.5 %all-gather.15.cloned.1.call-done.refs_0_.refs_1_ = bf16[104,128,128]{2,1,0:T(8,128)(2,1)} async-done(((bf16[26,128,128]{2,1,0:T(8,128)(2,1)}), bf16[104,128,128]{2,1,0:T(8,128)(2,1)}) %all-gather.15.cloned.1.call-update) | async-done | bytes 3407888 | tf_op jit(solution)/shard_map/all_gather | solution.py:413
  128.0 7.4 %collective-permute-done.15.refs_6_ = bf16[68,32,128]{2,1,0:T(8,128)(2,1)S(1)} collective-permute-done((bf16[68,32,128]{2,1,0:T(8,128)(2,1)S(1)}, bf16[68,32,128]{2,1,0:T(8,128)(2,1)S(1)}, u32[]{:S(2)}, u32[]{:S(2)}) %collective-permute-start.15) | collective-permute-done | bytes 557088 | tf_op jit(solution)/shard_map/ppermute | solution.py:31
  143.4 7.0 %collective-permute-done.8.refs_1_ = bf16[68,32,128]{2,1,0:T(8,128)(2,1)S(1)} collective-permute-done((bf16[68,32,128]{2,1,0:T(8,128)(2,1)}, bf16[68,32,128]{2,1,0:T(8,128)(2,1)S(1)}, u32[]{:S(2)}, u32[]{:S(2)}) %collective-permute-start.8) | collective-permute-done | bytes 557088 | tf_op jit(solution)/shard_map/ppermute | solution.py:31
  161.9 3.9 %collective-permute-done.10.refs_3_ = bf16[34,32,128]{2,1,0:T(8,128)(2,1)} collective-permute-done((bf16[34,32,128]{2,1,0:T(8,128)(2,1)}, bf16[34,32,128]{2,1,0:T(8,128)(2,1)}, u32[]{:S(2)}, u32[]{:S(2)}) %collective-permute-start.10) | collective-permute-done | bytes 278560 | tf_op jit(solution)/shard_map/ppermute | solution.py:34
  175.3 5.6 %first_sums.1 = (f32[2,2,32,128]{3,2,1,0:T(8,128)S(1)}, bf16[2048,32,128]{2,1,0:T(8,128)(2,1)}) custom-call(s32[7,64]{1,0:T(8,128)S(1)} %fusion.112.code_ref, s32[1]{0:T(128)} %bitcast.67.flag_ref, bf16[68,32,128]{2,1,0:T(8,128)(2,1)} %constant_dynamic-update-slice_fusion.14.refs_0_, bf16[68,32,128]{2,1,0:T(8,128)(2,1)S(1)} %collective-permute-done.8.refs_1_, ...), custom_call_target="tpu_custom_call" | custom-call | flops 134217728 | bytes 12582912 | tf_op jit(solution)/shard_map/first_sums/pallas_call | solution.py:59
  180.9 7.9 %all-gather.21.cloned.1.call-done.refs_5_ = bf16[80,128,128]{2,1,0:T(8,128)(2,1)} async-done(((bf16[20,128,128]{2,1,0:T(8,128)(2,1)}), bf16[80,128,128]{2,1,0:T(8,128)(2,1)}) %all-gather.21.cloned.1.call-update) | async-done | bytes 2621456 | tf_op jit(solution)/shard_map/all_gather | solution.py:413
  204.4 6.7 %all-to-all-start = ((bf16[16,2,32,128]{3,2,1,0:T(8,128)(2,1)}), bf16[16,2,32,128]{3,2,1,0:T(8,128)(2,1)S(1)}, u32[]{:S(2)}, u32[]{:S(2)}) async-start(bf16[16,2,32,128]{3,2,1,0:T(8,128)(2,1)} %get-tuple-element.172), calls=%async_computation | async-start | bytes 524288 | tf_op jit(solution)/shard_map/all_to_all | solution.py:482
  221.1 6.2 %all-to-all-start.1 = ((bf16[16,2,32,128]{3,2,1,0:T(8,128)(2,1)}), bf16[16,2,32,128]{3,2,1,0:T(8,128)(2,1)S(1)}, u32[]{:S(2)}, u32[]{:S(2)}) async-start(bf16[16,2,32,128]{3,2,1,0:T(8,128)(2,1)} %get-tuple-element.183), calls=%async_computation.1 | async-start | bytes 524288 | tf_op jit(solution)/shard_map/all_to_all | solution.py:482
  227.3 6.6 %known_sums.3.refs_5_ = f32[2,2,32,128]{3,2,1,0:T(8,128)S(1)} custom-call(s32[7,64]{1,0:T(8,128)S(1)} %fusion.112.code_ref, bf16[2048,32,128]{2,1,0:T(8,128)(2,1)} %get-tuple-element.185.store_ref, bf16[7,1,32,128,128]{4,3,2,1,0:T(8,128)(2,1)} %own_ref.5, bf16[7,1,32,128,128]{4,3,2,1,0:T(8,128)(2,1)} %collective-permute-done.19.refs_11_.other_ref), custom_call_target="tpu_custom_call" | custom-call | flops 134217728 | bytes 12582912 | tf_op jit(solution)/shard_map/known_sums/pallas_call | solution.py:59
  244.6 6.9 %all-to-all-start.2 = ((bf16[16,2,32,128]{3,2,1,0:T(8,128)(2,1)}), bf16[16,2,32,128]{3,2,1,0:T(8,128)(2,1)S(1)}, u32[]{:S(2)}, u32[]{:S(2)}) async-start(bf16[16,2,32,128]{3,2,1,0:T(8,128)(2,1)} %get-tuple-element.193), calls=%async_computation.2 | async-start | bytes 524288 | tf_op jit(solution)/shard_map/all_to_all | solution.py:482
  251.5 3.8 %middle_sum.8 = (f32[2,32,128]{2,1,0:T(8,128)S(1)}, bf16[48,128,128]{2,1,0:T(8,128)(2,1)S(1)}) custom-call(s32[2,14]{1,0:T(2,128)S(1)} %pad_add_fusion.2.counts_ref.refs_0_, s32[14,24]{1,0:T(8,128)S(1)} %fusion.102.fresh_ref.refs_1_, s32[14,52]{1,0:T(8,128)S(1)} %fusion.100.middle_ref, bf16[32,32,128]{2,1,0:T(8,128)(2,1)S(1)} %bitcast.221, ...), custom_call_target="tpu_custom_call" | custom-call | flops 41943040 | bytes 8388608 | tf_op jit(solution)/shard_map/middle_sum/pallas_call | solution.py:59
  255.3 3.7 %all-to-all-done.2 = bf16[16,2,32,128]{3,2,1,0:T(8,128)(2,1)S(1)} async-done(((bf16[16,2,32,128]{3,2,1,0:T(8,128)(2,1)}), bf16[16,2,32,128]{3,2,1,0:T(8,128)(2,1)S(1)}, u32[]{:S(2)}, u32[]{:S(2)}) %all-to-all-start.2) | async-done | bytes 262176 | tf_op jit(solution)/shard_map/all_to_all | solution.py:482
  265.2 7.0 %known_sums.4.refs_5_ = f32[2,2,32,128]{3,2,1,0:T(8,128)S(1)} custom-call(s32[7,64]{1,0:T(8,128)S(1)} %fusion.112.code_ref, bf16[2048,32,128]{2,1,0:T(8,128)(2,1)} %get-tuple-element.185.store_ref, bf16[7,1,32,128,128]{4,3,2,1,0:T(8,128)(2,1)} %own_ref.5, bf16[7,1,32,128,128]{4,3,2,1,0:T(8,128)(2,1)} %collective-permute-done.19.refs_11_.other_ref), custom_call_target="tpu_custom_call" | custom-call | flops 134217728 | bytes 12582912 | tf_op jit(solution)/shard_map/known_sums/pallas_call | solution.py:59
  276.2 4.7 %middle_sum.9 = (f32[2,32,128]{2,1,0:T(8,128)S(1)}, bf16[48,128,128]{2,1,0:T(8,128)(2,1)S(1)}) custom-call(s32[2,14]{1,0:T(2,128)S(1)} %pad_add_fusion.2.counts_ref.refs_0_, s32[14,24]{1,0:T(8,128)S(1)} %fusion.102.fresh_ref.refs_1_, s32[14,52]{1,0:T(8,128)S(1)} %fusion.100.middle_ref, bf16[32,32,128]{2,1,0:T(8,128)(2,1)S(1)} %bitcast.222, ...), custom_call_target="tpu_custom_call" | custom-call | flops 41943040 | bytes 8388608 | tf_op jit(solution)/shard_map/middle_sum/pallas_call | solution.py:59
  283.5 6.2 %all-to-all-start.4 = ((bf16[16,2,32,128]{3,2,1,0:T(8,128)(2,1)}), bf16[16,2,32,128]{3,2,1,0:T(8,128)(2,1)S(1)}, u32[]{:S(2)}, u32[]{:S(2)}) async-start(bf16[16,2,32,128]{3,2,1,0:T(8,128)(2,1)} %get-tuple-element.208), calls=%async_computation.4 | async-start | bytes 524288 | tf_op jit(solution)/shard_map/all_to_all | solution.py:482
  289.7 4.8 %known_sums.5.refs_5_ = f32[1,2,32,128]{3,2,1,0:T(8,128)} custom-call(s32[7,64]{1,0:T(8,128)S(1)} %fusion.112.code_ref, bf16[2048,32,128]{2,1,0:T(8,128)(2,1)} %get-tuple-element.185.store_ref, bf16[7,1,32,128,128]{4,3,2,1,0:T(8,128)(2,1)} %own_ref.5, bf16[7,1,32,128,128]{4,3,2,1,0:T(8,128)(2,1)} %collective-permute-done.19.refs_11_.other_ref), custom_call_target="tpu_custom_call" | custom-call | flops 67108864 | bytes 6291456 | tf_op jit(solution)/shard_map/known_sums/pallas_call | solution.py:59
  299.8 5.5 %middle_sum.10 = (f32[2,32,128]{2,1,0:T(8,128)S(1)}, bf16[48,128,128]{2,1,0:T(8,128)(2,1)S(1)}) custom-call(s32[2,14]{1,0:T(2,128)S(1)} %copy-done.8, s32[14,24]{1,0:T(8,128)S(1)} %fusion.102.fresh_ref.refs_1_, s32[14,52]{1,0:T(8,128)S(1)} %fusion.100.middle_ref, bf16[32,32,128]{2,1,0:T(8,128)(2,1)S(1)} %bitcast.223, bf16[32,32,128]{2,1,0:T(8,128)(2,1)S(1)} %bitcast.228, ...), custom_call_target="tpu_custom_call" | custom-call | flops 41943040 | bytes 8388608 | tf_op jit(solution)/shard_map/middle_sum/pallas_call | solution.py:59
  310.9 7.3 %all-to-all-start.5 = ((bf16[16,2,32,128]{3,2,1,0:T(8,128)(2,1)}), bf16[16,2,32,128]{3,2,1,0:T(8,128)(2,1)S(1)}, u32[]{:S(2)}, u32[]{:S(2)}) async-start(bf16[16,2,32,128]{3,2,1,0:T(8,128)(2,1)} %copy-done.6), calls=%async_computation.5 | async-start | bytes 524288 | tf_op jit(solution)/shard_map/all_to_all | solution.py:482
  323.2 6.3 %middle_sum.11 = (f32[2,32,128]{2,1,0:T(8,128)S(1)}, bf16[48,128,128]{2,1,0:T(8,128)(2,1)S(1)}) custom-call(s32[2,14]{1,0:T(2,128)S(1)} %copy-done.10, s32[14,24]{1,0:T(8,128)S(1)} %fusion.102.fresh_ref.refs_1_, s32[14,52]{1,0:T(8,128)S(1)} %fusion.100.middle_ref, bf16[32,32,128]{2,1,0:T(8,128)(2,1)S(1)} %bitcast.224, bf16[32,32,128]{2,1,0:T(8,128)(2,1)S(1)} %bitcast.229, ...), custom_call_target="tpu_custom_call" | custom-call | flops 41943040 | bytes 8388608 | tf_op jit(solution)/shard_map/middle_sum/pallas_call | solution.py:59
  331.6 14.0 %solve_level.13 = bf16[2,32,128]{2,1,0:T(8,128)(2,1)S(1)} custom-call(s32[2,14]{1,0:T(2,128)S(1)} %copy-done.11, s32[14,24]{1,0:T(8,128)S(1)} %fusion.102.fresh_ref.refs_1_, f32[2,32,128]{2,1,0:T(8,128)S(1)} %copy-done.13, bf16[48,128,128]{2,1,0:T(8,128)(2,1)S(1)} %get-tuple-element.214.refs_3_, bf16[32,32,128]{2,1,0:T(8,128)(2,1)S(1)} %bitcast.239, ...), custom_call_target="tpu_custom_call" | custom-call | tf_op jit(solution)/shard_map/solve_level/pallas_call | solution.py:59
  346.3 10.0 %collective-permute-start.38 = (bf16[7,32,128]{2,1,0:T(8,128)(2,1)}, bf16[7,32,128]{2,1,0:T(8,128)(2,1)S(1)}, u32[]{:S(2)}, u32[]{:S(2)}) collective-permute-start(bf16[7,32,128]{2,1,0:T(8,128)(2,1)} %get-tuple-element.283), channel_id=1, source_target_pairs={{0,4},{4,0},{1,5},{5,1},{2,6},{6,2},{3,7},{7,3},{8,12},{12,8},{9,1... | collective-permute-start | bytes 172040 | tf_op jit(solution)/shard_map/ppermute | solution.py:23
  (226 shorter events, 132.6 us)
Async XLA Ops:
  7.4 64.9 %all-gather.17.cloned.1.call-start = ((), (), s32[]{:S(2)}) async-start(), calls=%async_computation.8 | async-start | bytes 5570560 | tf_op jit(solution)/shard_map/all_gather | solution.py:413
  18.5 97.6 %all-gather.15.cloned.1.call-start = ((), (), s32[]{:S(2)}) async-start(), calls=%async_computation.7 | async-start | bytes 4259840 | tf_op jit(solution)/shard_map/all_gather | solution.py:413
  19.2 151.2 %all-gather.19.cloned.1.call-start = ((), (), s32[]{:S(2)}) async-start(), calls=%async_computation.9 | async-start | bytes 3112960 | tf_op jit(solution)/shard_map/all_gather | solution.py:413
  20.0 168.9 %all-gather.21.cloned.1.call-start = ((), (), s32[]{:S(2)}) async-start(), calls=%async_computation.10 | async-start | bytes 3276800 | tf_op jit(solution)/shard_map/all_gather | solution.py:413
  23.5 147.7 %collective-permute-start.19 = (bf16[7,1,32,128,128]{4,3,2,1,0:T(8,128)(2,1)}, bf16[7,1,32,128,128]{4,3,2,1,0:T(8,128)(2,1)}, u32[]{:S(2)}, u32[]{:S(2)}) collective-permute-start(bf16[7,1,32,128,128]{4,3,2,1,0:T(8,128)(2,1)} %own_ref.5), channel_id=1, source_target_pairs={{0,4},{4,0},{1,5},{5,1},{2,6},{6,2},{3,7},{7,3},{8,12},{12,8},{9,1... | collective-permute-start | bytes 22020104 | tf_op jit(solution)/shard_map/ppermute | solution.py:23
  29.8 45.0 %collective-permute-start.1 = (s32[7,2,32]{2,0,1:T(8,128)S(1)}, s32[7,2,32]{2,0,1:T(8,128)S(1)}, u32[]{:S(2)}, u32[]{:S(2)}) collective-permute-start(s32[7,2,32]{2,0,1:T(8,128)S(1)} %get-tuple-element.297), channel_id=1, source_target_pairs={{0,1},{1,0},{2,3},{3,2},{4,5},{5,4},{6,7},{7,6},{8,9},{9,8},{10,11... | collective-permute-start | bytes 5384 | tf_op jit(solution)/shard_map/ppermute | solution.py:438
  31.1 47.7 %collective-permute-start.12 = (bf16[17,32,128]{2,1,0:T(8,128)(2,1)S(1)}, bf16[17,32,128]{2,1,0:T(8,128)(2,1)S(1)}, u32[]{:S(2)}, u32[]{:S(2)}) collective-permute-start(bf16[17,32,128]{2,1,0:T(8,128)(2,1)S(1)} %collective-permute-done.4), channel_id=1, source_target_pairs={{0,8},{8,0},{16,24},{24,16},{1,9},{9,1},{17,25},{25,17},{2,10},{10... | collective-permute-start | bytes 417800 | tf_op jit(solution)/shard_map/ppermute | solution.py:27
  72.3 179.3 %collective-permute-start.29 = (bf16[136,128,128]{2,1,0:T(8,128)(2,1)}, bf16[136,128,128]{2,1,0:T(8,128)(2,1)}, u32[]{:S(2)}, u32[]{:S(2)}) collective-permute-start(bf16[136,128,128]{2,1,0:T(8,128)(2,1)} %all-gather.17.cloned.1.call-done.refs_2_.refs_3_), channel_id=1, source_target_pairs={{0,4},{4,0},{1,5},{5,1},{2,6},{6,2},{3,7},{7,3},{8,12},{12,8},{9,1... | collective-permute-start | bytes 13369352 | tf_op jit(solution)/shard_map/ppermute | solution.py:23
  81.7 35.0 %collective-permute-start.5 = (bf16[17,32,128]{2,1,0:T(8,128)(2,1)S(1)}, bf16[17,32,128]{2,1,0:T(8,128)(2,1)S(1)}, u32[]{:S(2)}, u32[]{:S(2)}) collective-permute-start(bf16[17,32,128]{2,1,0:T(8,128)(2,1)S(1)} %get-tuple-element.167), channel_id=1, source_target_pairs={{0,32},{32,0},{64,96},{96,64},{1,33},{33,1},{65,97},{97,65},{2,34}... | collective-permute-start | bytes 417800 | tf_op jit(solution)/shard_map/ppermute | solution.py:27
  83.0 36.5 %collective-permute-start.6 = (bf16[17,32,128]{2,1,0:T(8,128)(2,1)S(1)}, bf16[17,32,128]{2,1,0:T(8,128)(2,1)S(1)}, u32[]{:S(2)}, u32[]{:S(2)}) collective-permute-start(bf16[17,32,128]{2,1,0:T(8,128)(2,1)S(1)} %get-tuple-element.167), channel_id=1, source_target_pairs={{0,64},{32,96},{64,0},{96,32},{1,65},{33,97},{65,1},{97,33},{2,66}... | collective-permute-start | bytes 417800 | tf_op jit(solution)/shard_map/ppermute | solution.py:27
  116.0 96.6 %collective-permute-start.25 = (bf16[104,128,128]{2,1,0:T(8,128)(2,1)}, bf16[104,128,128]{2,1,0:T(8,128)(2,1)}, u32[]{:S(2)}, u32[]{:S(2)}) collective-permute-start(bf16[104,128,128]{2,1,0:T(8,128)(2,1)} %all-gather.15.cloned.1.call-done.refs_0_.refs_1_), channel_id=1, source_target_pairs={{0,4},{4,0},{1,5},{5,1},{2,6},{6,2},{3,7},{7,3},{8,12},{12,8},{9,1... | collective-permute-start | bytes 10223624 | tf_op jit(solution)/shard_map/ppermute | solution.py:23
  119.5 15.9 %collective-permute-start.15 = (bf16[68,32,128]{2,1,0:T(8,128)(2,1)S(1)}, bf16[68,32,128]{2,1,0:T(8,128)(2,1)S(1)}, u32[]{:S(2)}, u32[]{:S(2)}) collective-permute-start(bf16[68,32,128]{2,1,0:T(8,128)(2,1)S(1)} %constant_dynamic-update-slice_fusion.18.refs_5_), channel_id=1, source_target_pairs={{0,32},{32,64},{64,96},{96,0},{1,33},{33,65},{65,97},{97,1},{2,34}... | collective-permute-start | bytes 1671176 | tf_op jit(solution)/shard_map/ppermute | solution.py:31
  135.4 15.0 %collective-permute-start.8 = (bf16[68,32,128]{2,1,0:T(8,128)(2,1)}, bf16[68,32,128]{2,1,0:T(8,128)(2,1)S(1)}, u32[]{:S(2)}, u32[]{:S(2)}) collective-permute-start(bf16[68,32,128]{2,1,0:T(8,128)(2,1)} %constant_dynamic-update-slice_fusion.14.refs_0_), channel_id=1, source_target_pairs={{0,8},{8,16},{16,24},{24,0},{1,9},{9,17},{17,25},{25,1},{2,10},{10... | collective-permute-start | bytes 1671176 | tf_op jit(solution)/shard_map/ppermute | solution.py:31
  137.2 14.6 %collective-permute-start.9 = (bf16[68,32,128]{2,1,0:T(8,128)(2,1)}, bf16[68,32,128]{2,1,0:T(8,128)(2,1)S(1)}, u32[]{:S(2)}, u32[]{:S(2)}) collective-permute-start(bf16[68,32,128]{2,1,0:T(8,128)(2,1)} %constant_dynamic-update-slice_fusion.14.refs_0_), channel_id=1, source_target_pairs={{0,24},{8,0},{16,8},{24,16},{1,25},{9,1},{17,9},{25,17},{2,26},{10... | collective-permute-start | bytes 1671176 | tf_op jit(solution)/shard_map/ppermute | solution.py:32
  165.8 23.7 %collective-permute-start.24 = (bf16[8,1,128,128]{3,2,1,0:T(8,128)(2,1)}, bf16[8,1,128,128]{3,2,1,0:T(8,128)(2,1)S(1)}, u32[]{:S(2)}, u32[]{:S(2)}) collective-permute-start(bf16[8,1,128,128]{3,2,1,0:T(8,128)(2,1)} %refs_10_.13), channel_id=1, source_target_pairs={{0,4},{4,0},{1,5},{5,1},{2,6},{6,2},{3,7},{7,3},{8,12},{12,8},{9,1... | collective-permute-start | bytes 786440 | tf_op jit(solution)/shard_map/ppermute | solution.py:23
  170.5 129.3 %collective-permute-start.33 = (bf16[76,128,128]{2,1,0:T(8,128)(2,1)}, bf16[76,128,128]{2,1,0:T(8,128)(2,1)}, u32[]{:S(2)}, u32[]{:S(2)}) collective-permute-start(bf16[76,128,128]{2,1,0:T(8,128)(2,1)} %all-gather.19.cloned.1.call-done.refs_4_), channel_id=1, source_target_pairs={{0,4},{4,0},{1,5},{5,1},{2,6},{6,2},{3,7},{7,3},{8,12},{12,8},{9,1... | collective-permute-start | bytes 7471112 | tf_op jit(solution)/shard_map/ppermute | solution.py:23
  188.9 132.0 %collective-permute-start.34 = (bf16[80,128,128]{2,1,0:T(8,128)(2,1)}, bf16[80,128,128]{2,1,0:T(8,128)(2,1)}, u32[]{:S(2)}, u32[]{:S(2)}) collective-permute-start(bf16[80,128,128]{2,1,0:T(8,128)(2,1)} %all-gather.21.cloned.1.call-done.refs_5_), channel_id=1, source_target_pairs={{0,4},{4,0},{1,5},{5,1},{2,6},{6,2},{3,7},{7,3},{8,12},{12,8},{9,1... | collective-permute-start | bytes 7864328 | tf_op jit(solution)/shard_map/ppermute | solution.py:23
  221.1 20.9 %all-to-all-start.1 = ((bf16[16,2,32,128]{3,2,1,0:T(8,128)(2,1)}), bf16[16,2,32,128]{3,2,1,0:T(8,128)(2,1)S(1)}, u32[]{:S(2)}, u32[]{:S(2)}) async-start(bf16[16,2,32,128]{3,2,1,0:T(8,128)(2,1)} %get-tuple-element.183), calls=%async_computation.1 | async-start | bytes 524288 | tf_op jit(solution)/shard_map/all_to_all | solution.py:482
  261.7 19.2 %all-to-all-start.3 = ((bf16[16,2,32,128]{3,2,1,0:T(8,128)(2,1)}), bf16[16,2,32,128]{3,2,1,0:T(8,128)(2,1)S(1)}, u32[]{:S(2)}, u32[]{:S(2)}) async-start(bf16[16,2,32,128]{3,2,1,0:T(8,128)(2,1)} %get-tuple-element.199), calls=%async_computation.3 | async-start | bytes 524288 | tf_op jit(solution)/shard_map/all_to_all | solution.py:482
  283.5 22.4 %all-to-all-start.4 = ((bf16[16,2,32,128]{3,2,1,0:T(8,128)(2,1)}), bf16[16,2,32,128]{3,2,1,0:T(8,128)(2,1)S(1)}, u32[]{:S(2)}, u32[]{:S(2)}) async-start(bf16[16,2,32,128]{3,2,1,0:T(8,128)(2,1)} %get-tuple-element.208), calls=%async_computation.4 | async-start | bytes 524288 | tf_op jit(solution)/shard_map/all_to_all | solution.py:482
  294.6 35.5 %collective-permute-start.35 = (f32[1,2,32,128]{3,2,1,0:T(8,128)}, f32[1,2,32,128]{3,2,1,0:T(8,128)}, u32[]{:S(2)}, u32[]{:S(2)}) collective-permute-start(f32[1,2,32,128]{3,2,1,0:T(8,128)} %known_sums.5.refs_5_), channel_id=1, source_target_pairs={{0,1},{1,0},{2,3},{3,2},{4,5},{5,4},{6,7},{7,6},{8,9},{9,8},{10,11... | collective-permute-start | bytes 98312 | tf_op jit(solution)/shard_map/ppermute | solution.py:466
  294.7 35.5 %collective-permute-start.36 = (f32[1,2,32,128]{3,2,1,0:T(8,128)}, f32[1,2,32,128]{3,2,1,0:T(8,128)}, u32[]{:S(2)}, u32[]{:S(2)}) collective-permute-start(f32[1,2,32,128]{3,2,1,0:T(8,128)} %known_sums.5.refs_5_), channel_id=1, source_target_pairs={{0,2},{1,3},{2,0},{3,1},{4,6},{5,7},{6,4},{7,5},{8,10},{9,11},{10,... | collective-permute-start | bytes 98312 | tf_op jit(solution)/shard_map/ppermute | solution.py:466
  297.8 32.3 %collective-permute-start.37 = (f32[1,2,32,128]{3,2,1,0:T(8,128)}, f32[1,2,32,128]{3,2,1,0:T(8,128)}, u32[]{:S(2)}, u32[]{:S(2)}) collective-permute-start(f32[1,2,32,128]{3,2,1,0:T(8,128)} %known_sums.5.refs_5_), channel_id=1, source_target_pairs={{0,3},{1,2},{2,1},{3,0},{4,7},{5,6},{6,5},{7,4},{8,11},{9,10},{10,... | collective-permute-start | bytes 98312 | tf_op jit(solution)/shard_map/ppermute | solution.py:466
  310.9 19.3 %all-to-all-start.5 = ((bf16[16,2,32,128]{3,2,1,0:T(8,128)(2,1)}), bf16[16,2,32,128]{3,2,1,0:T(8,128)(2,1)S(1)}, u32[]{:S(2)}, u32[]{:S(2)}) async-start(bf16[16,2,32,128]{3,2,1,0:T(8,128)(2,1)} %copy-done.6), calls=%async_computation.5 | async-start | bytes 524288 | tf_op jit(solution)/shard_map/all_to_all | solution.py:482
  (55 other events, 978.4 us)
Sparse Core Ops, SparseCore 0:
  18.6 53.6 all-gather.16
  73.9 42.0 all-gather.14
  117.7 34.2 all-gather.18
  153.6 35.2 all-gather.20
Sparse Core Ops, SparseCore 1:
  174.4 2.5 sort.21.cloned.1.call-done
  190.4 2.5 sort.23.cloned.1.call-done
  (2 shorter events, 0.0 us)

commit v3 on v2

--- a/solution.py
+++ b/solution.py
@@ -42,7 +42,8 @@
 
 GROUP = 8
 UNROLL = 4
-CAPACITY = (12, 14, 16, 18, 19, 20)
+LATE_LIMIT = 60 * 1024 * 1024
+CAPACITY = (10, 12, 14, 16, 17, 18)
 FRESH_CAPACITY = 24
 MIDDLE_CAPACITY = 52
 CHUNKS = ((2, 3), (4, 5), (6,), (7,))
@@ -55,14 +56,14 @@
             return n, before, sum(CAPACITY[one - 2] for one in chunk)
 
 
-def call(kernel, name, operands, in_spaces, outs, out_spaces, scratch, flops=0, bytes_accessed=0):
+def call(kernel, name, operands, in_spaces, outs, out_spaces, scratch, flops=0, bytes_accessed=0, limit=VMEM_LIMIT):
     return pl.pallas_call(
         kernel,
         out_shape=outs,
         in_specs=[pl.BlockSpec(memory_space=space) for space in in_spaces],
         out_specs=[pl.BlockSpec(memory_space=space) for space in out_spaces],
         scratch_shapes=scratch,
-        compiler_params=pltpu.CompilerParams(vmem_limit_bytes=VMEM_LIMIT),
+        compiler_params=pltpu.CompilerParams(vmem_limit_bytes=limit),
         cost_estimate=pl.CostEstimate(flops=flops, bytes_accessed=bytes_accessed, transcendentals=0),
         name=name,
     )(*operands)
@@ -98,9 +99,17 @@
             pltpu.make_async_copy(a_ref.at[level - 1, 0], target, block_sems.at[n, r]).start()
 
 
+def send_copies(source, copies_ref, sems):
+    sends = [pltpu.make_async_copy(source, copies_ref.at[i], sems.at[i]) for i in range(copies_ref.shape[0])]
+    for send in sends:
+        send.start()
+    for send in sends:
+        send.wait()
+
+
 def first_kernel(levels, code_ref, flag_ref, *refs):
-    sources, refs = refs[:-9], refs[-9:]
-    own_ref, other_ref, out_ref, store_ref, blocks, block_sems, pack_sems, packed, store_sem = refs
+    sources, refs = refs[:-11], refs[-11:]
+    own_ref, other_ref, copies_ref, store_ref, blocks, block_sems, out_ref, copy_sems, pack_sems, packed, store_sem = refs
     start_blocks(levels, own_ref, other_ref, blocks, block_sems)
     packs, start = [], 0
     for i, source in enumerate(sources):
@@ -117,10 +126,13 @@
             level, code_ref, lambda k, code: packed[code], own_ref, other_ref, out_ref.at[n], blocks.at[n], block_sems.at[n]
         )
     out_ref[0] = out_ref[0] + jnp.where(flag_ref[0] > 0, jnp.float32(jnp.nan), jnp.float32(0.0))
+    send_copies(out_ref, copies_ref, copy_sems)
     keep.wait()
 
 
-def known_kernel(levels, code_ref, store_ref, own_ref, other_ref, out_ref, blocks, block_sems, picked, pick_sem):
+def known_kernel(
+    levels, code_ref, store_ref, own_ref, other_ref, copies_ref, blocks, block_sems, out_ref, copy_sems, picked, pick_sem
+):
     slots = code_ref.shape[1]
     start_blocks(levels, own_ref, other_ref, blocks, block_sems)
     for n, level in enumerate(levels):
@@ -135,12 +147,18 @@
     for n, level in enumerate(levels):
         picks = lambda k, code, n=n: picked[n * slots + k]
         gather_sum(level, code_ref, picks, own_ref, other_ref, out_ref.at[n], blocks.at[n], block_sems.at[n])
+    send_copies(out_ref, copies_ref, copy_sems)
 
 
 def known_sums(levels, code, flag, sources, own, other):
     slots, one, some = code.shape[1], sources[0].shape[1:], len(levels)
-    sums = jax.ShapeDtypeStruct((some, 2) + one, jnp.float32)
-    scratch = [pltpu.VMEM((some, slots, one[1], one[1]), jnp.bfloat16), pltpu.SemaphoreType.DMA((some, 2))]
+    sums = jax.ShapeDtypeStruct((4, some, 2) + one, jnp.float32)
+    scratch = [
+        pltpu.VMEM((some, slots, one[1], one[1]), jnp.bfloat16),
+        pltpu.SemaphoreType.DMA((some, 2)),
+        pltpu.VMEM((some, 2) + one, jnp.float32),
+        pltpu.SemaphoreType.DMA((4,)),
+    ]
     cost = dict(
         flops=2 * some * slots * one[0] * one[1] * one[1], bytes_accessed=some * slots * one[1] * (one[1] + 2 * one[0]) * 4
     )
@@ -149,7 +167,7 @@
         scratch += [pltpu.VMEM((some * slots,) + one, jnp.bfloat16), pltpu.SemaphoreType.DMA]
         kernel = functools.partial(known_kernel, levels)
         operands = (code, *sources, own, other)
-        return call(kernel, "known_sums", operands, [pltpu.SMEM] + spaces, [sums], [pltpu.VMEM], scratch, **cost)[0]
+        return call(kernel, "known_sums", operands, [pltpu.SMEM] + spaces, [sums], [pltpu.HBM], scratch, limit=LATE_LIMIT, **cost)[0]
     known = sum(v.shape[0] for v in sources)
     scratch += [
         pltpu.SemaphoreType.DMA((len(sources),)),
@@ -160,66 +178,45 @@
     kernel = functools.partial(first_kernel, levels)
     operands = (code, flag, *sources, own, other)
     spaces = [pltpu.SMEM] * 2 + spaces
-    return call(kernel, "first_sums", operands, spaces, [sums, store], [pltpu.VMEM, pltpu.HBM], scratch, **cost)
-
-
-def near_kernel(rank_ref, off_ref, *refs):
-    outs, (blocks, sem, out_sems) = refs[: len(CHUNKS)], refs[len(CHUNKS) :]
+    return call(kernel, "first_sums", operands, spaces, [sums, store], [pltpu.HBM, pltpu.HBM], scratch, **cost)
+
+
+def near_kernel(levels, rank_ref, off_ref, out_ref, blocks, sem, out_sem):
     slots = rank_ref.shape[1]
-    places = []
-    for level in range(2, 2 + len(CAPACITY)):
-        n, before, _ = chunk_of(level)
-        places.append(sum(sum(CAPACITY[one - 2] for one in chunk) for chunk in CHUNKS[:n]) + before)
-        if before == 0:
-            blocks[places[-1]] = jnp.zeros(blocks.shape[1:], blocks.dtype)
-
-    for level, place in zip(range(2, 2 + len(CAPACITY)), places):
-
-        def copy_of(k, level=level, place=place):
-            target = place + rank_ref[level - 1, k]
-            return pltpu.make_async_copy(off_ref.at[level - 1, 0, k], blocks.at[target], sem.at[target])
-
-        def load(k, carry, level=level, copy_of=copy_of):
-            @pl.when(rank_ref[level - 1, k] >= 0)
-            def _():
-                copy_of(k).start()
-
-            return carry
-
-        lax.fori_loop(0, slots, load, 0)
-
-    for level, place in zip(range(2, 2 + len(CAPACITY)), places):
-
-        def wait(k, carry, level=level, place=place):
-            @pl.when(rank_ref[level - 1, k] >= 0)
-            def _():
-                target = place + rank_ref[level - 1, k]
-                pltpu.make_async_copy(off_ref.at[level - 1, 0, k], blocks.at[target], sem.at[target]).wait()
-
-            return carry
-
-        lax.fori_loop(0, slots, wait, 0)
-    start, stores = 0, []
-    for n, out in enumerate(outs):
-        stores.append(pltpu.make_async_copy(blocks.at[pl.ds(start, out.shape[0])], out, out_sems.at[n]))
-        stores[-1].start()
-        start += out.shape[0]
-    for store in stores:
-        store.wait()
-
-
-def near_blocks(rank, off):
+    blocks[0] = jnp.zeros(blocks.shape[1:], blocks.dtype)
+
+    def each(do):
+        for level in levels:
+            place = chunk_of(level)[1]
+
+            def body(k, carry, level=level, place=place):
+                @pl.when(rank_ref[level - 1, k] >= 0)
+                def _():
+                    target = place + rank_ref[level - 1, k]
+                    do(pltpu.make_async_copy(off_ref.at[level - 1, 0, k], blocks.at[target], sem.at[target]))
+
+                return carry
+
+            lax.fori_loop(0, slots, body, 0)
+
+    each(lambda copy: copy.start())
+    each(lambda copy: copy.wait())
+    store = pltpu.make_async_copy(blocks, out_ref, out_sem)
+    store.start()
+    store.wait()
+
+
+def near_blocks(chunk, rank, off):
     block = off.shape[-1]
-    sizes = [sum(CAPACITY[one - 2] for one in chunk) for chunk in CHUNKS]
-    outs = [jax.ShapeDtypeStruct((size, block, block), jnp.bfloat16) for size in sizes]
+    size = sum(CAPACITY[one - 2] for one in chunk)
+    out = jax.ShapeDtypeStruct((size, block, block), jnp.bfloat16)
     scratch = [
-        pltpu.VMEM((sum(sizes), block, block), jnp.bfloat16),
-        pltpu.SemaphoreType.DMA((sum(sizes),)),
-        pltpu.SemaphoreType.DMA((len(sizes),)),
+        pltpu.VMEM((size, block, block), jnp.bfloat16),
+        pltpu.SemaphoreType.DMA((size,)),
+        pltpu.SemaphoreType.DMA,
     ]
-    return call(
-        near_kernel, "near_blocks", (rank, off), [pltpu.SMEM, pltpu.HBM], outs, [pltpu.HBM] * len(sizes), scratch
-    )
+    kernel = functools.partial(near_kernel, chunk)
+    return call(kernel, "near_blocks", (rank, off), [pltpu.SMEM, pltpu.HBM], [out], [pltpu.HBM], scratch)[0]
 
 
 def add_listed(total, count, entry_of, block_of, solved_of, ready=None):
@@ -306,7 +303,7 @@
     operands = (counts, fresh, middle, *solved, own, other)
     kernel = functools.partial(middle_kernel, level)
     return call(
-        kernel, "middle_sum", operands, spaces, outs, [pltpu.VMEM] * 2, scratch, 2 * 40 * rhs_cols * block**2, 8 << 20
+        kernel, "middle_sum", operands, spaces, outs, [pltpu.VMEM] * 2, scratch, 2 * 40 * rhs_cols * block**2, 8 << 20, LATE_LIMIT
     )
 
 
@@ -314,9 +311,9 @@
     near = level > 1
     if near:
         (counts_ref, fresh_ref, middle_ref, near_ref, solved_ref), refs = refs[:5], refs[5:]
-    p0, p1, p2, p3, rhs_ref, own_d_ref, other_d_ref, out_ref = refs[:8]
+    sums, rhs_ref, own_d_ref, other_d_ref, out_ref = refs[:5]
     for r, d_ref in enumerate((own_d_ref, other_d_ref)):
-        coupled = (p0[at, r] + p1[at, r]) + (p2[at, r] + p3[at, r])
+        coupled = (sums[0, at, r] + sums[1, at, r]) + (sums[2, at, r] + sums[3, at, r])
         if near:
             row = 2 * (level - 1) + r
             first = level - 2
@@ -333,27 +330,23 @@
         solved = nt_dot(reduced, d_ref[level, 0]).astype(jnp.bfloat16)
         out_ref[r] = solved
         if not last:
-            refs[9][lax.axis_index("core") ^ r] = solved
+            refs[6][lax.axis_index("core") ^ r] = solved
     if not last:
-        all_ref, both, sems = refs[8:]
-        sends = [pltpu.make_async_copy(both, all_ref.at[i], sems.at[i]) for i in range(all_ref.shape[0])]
-        for send in sends:
-            send.start()
-        for send in sends:
-            send.wait()
-
-
-def solve_level(level, at, near, partials, rhs, own_d, other_d, copies):
-    one = partials[0].shape[2:]
+        all_ref, both, sems = refs[5:]
+        send_copies(both, all_ref, sems)
+
+
+def solve_level(level, at, near, sums, rhs, own_d, other_d, copies):
+    one = sums.shape[3:]
     outs, spaces, scratch = [jax.ShapeDtypeStruct((2,) + one, jnp.bfloat16)], [pltpu.VMEM], []
     if copies:
         outs.append(jax.ShapeDtypeStruct((copies, 2) + one, jnp.bfloat16))
         spaces.append(pltpu.HBM)
         scratch = [pltpu.VMEM((2,) + one, jnp.bfloat16), pltpu.SemaphoreType.DMA((copies,))]
-    in_spaces = ([pltpu.SMEM] * 2 + [pltpu.VMEM] * 3 if near else []) + [pltpu.VMEM] * 7
+    in_spaces = ([pltpu.SMEM] * 2 + [pltpu.VMEM] * 3 if near else []) + [pltpu.VMEM] * 4
     kernel = functools.partial(solve_kernel, level, at, not copies)
     return call(
-        kernel, "solve_level", (*near, *partials, rhs, own_d, other_d), in_spaces, outs, spaces, scratch
+        kernel, "solve_level", (*near, sums, rhs, own_d, other_d), in_spaces, outs, spaces, scratch, limit=LATE_LIMIT
     )
 
 
@@ -409,9 +402,13 @@
     limits = jnp.array((0,) + CAPACITY, jnp.int32)[:, None]
     own_rank = jnp.cumsum(own_inside.astype(jnp.int32), axis=1) - 1
     own_rank = jnp.where(own_inside & (own_rank < limits), own_rank, -1)
-    nears = near_blocks(own_rank, off_blocks)
+    own_rank, known_own = tied(own_rank, known_own)
+    nears = [near_blocks(chunk, own_rank, off_blocks) for chunk in CHUNKS]
     near_own = [lax.all_gather(v, "x", axis=0, tiled=True) for v in nears]
-    near_other = [swap_cores(v) for v in near_own]
+    near_other = {}
+
+    def swap_chunk(n, after):
+        near_other[n] = swap_cores(tied(near_own[n], after)[0])
 
     code_both = jnp.stack([code_own, swap_cores(code_own)], axis=1)
     rhs_both = jnp.concatenate([my_half(rhs, 2), swap_cores(their_half(rhs, 2))], axis=1)
@@ -434,8 +431,10 @@
     slot_of = jnp.where(away == 3, 1, jnp.where(away == 1, 2, jnp.where(away == 2, 3, 0)))
     known_place = jnp.where(mine_too, 0, 16 * each) + slot_of * (4 * each) + place
     known_code = jnp.where(keep & (index < outer + 32), known_place, -1).reshape(levels - 1, -1)
-
-    every = jnp.stack([code_both] + [lax.ppermute(code_both, "x", xor_pairs(4, k)) for k in (1, 2, 3)], axis=2)
+    known_code, _ = tied(known_code, nears)
+
+    code_late, _ = tied(code_both, color_a[1])
+    every = jnp.stack([code_both] + [lax.ppermute(code_late, "x", xor_pairs(4, k)) for k in (1, 2, 3)], axis=2)
     this = jnp.arange(levels - 1)[:, None, None, None]
     every_inside = (every >= 1024 + outer + 32) & (this > 0)
     rank = jnp.cumsum(every_inside.astype(jnp.int32), axis=3) - 1
@@ -463,35 +462,37 @@
     fresh_list, middle_list = jnp.maximum(fresh_list, 0), jnp.maximum(middle_list, 0)
 
     def over_x(value):
-        return [value] + [lax.ppermute(value, "x", xor_pairs(4, k)) for k in (1, 2, 3)]
+        return lax.all_to_all(value, "x", 0, 0)
 
     batches = ((1, 2), (3, 4), (5, 6), (7,))
     value, store = known_sums(batches[0], known_code, flag, color_a + color_b, off_blocks, off_other)
-    sums = {level: (over_x_value, n) for over_x_value in [over_x(value)] for n, level in enumerate(batches[0])}
-    own_rows, other_rows, solved_levels, pending = [], [], [], None
-    near = ()
+    swap_chunk(0, value)
+    spread = over_x(value)
+    sums = {level: (spread, n) for n, level in enumerate(batches[0])}
+    own_rows, other_rows, solved_levels, near = [], [], [], ()
     for level in range(1, levels):
         last = level == levels - 1
-        partials, at = sums[level]
-        outs = solve_level(level, at, near, partials, rhs_both, diag_inv, diag_other, 0 if last else 16)
+        spread, at = sums[level]
+        outs = solve_level(level, at, near, spread, rhs_both, diag_inv, diag_other, 0 if last else 16)
         own_rows.append(outs[0][0])
         other_rows.append(outs[0][1])
         if last:
             break
-        tie, sent = tied(counts, outs[1])
+        counts_now, sent = tied(counts, outs[1])
         solved = lax.all_to_all(sent, ("z", "y"), 0, 0).reshape(32, half, block)
-        if pending is not None:
-            batch, value = pending
-            value, _ = tied(value, sent)
-            spread = over_x(value)
+        if level % 2 == 1 and level // 2 + 1 < len(batches):
+            batch = batches[level // 2 + 1]
+            value = known_sums(batch, tied(known_code, sent)[0], None, [store], off_blocks, off_other)
+            solved, value = tied(solved, value)
+        elif level % 2 == 0:
+            spread = over_x(tied(value, sent)[0])
             sums.update({one: (spread, n) for n, one in enumerate(batch)})
-            pending = None
-        if level < len(batches):
-            code, _ = tied(known_code, sent)
-            pending = (batches[level], known_sums(batches[level], code, None, [store], off_blocks, off_other))
+        for n, chunk in enumerate(CHUNKS):
+            if n > 0 and chunk[0] == level + 2:
+                swap_chunk(n, sent)
         n = chunk_of(level + 1)[0]
         middle, near_now = middle_sum(
-            level + 1, tie, fresh_list, middle_list, solved_levels, near_own[n], near_other[n], half
+            level + 1, counts_now, fresh_list, middle_list, solved_levels, near_own[n], near_other[n], half
         )
         near = (counts, fresh_list, middle, near_now, solved)
         solved_levels = solved_levels + [solved]

time: 371 us -> 303 us (0.82)
  waiting for transfers between devices: 126 us -> 53.6 us
  blocking collectives: 0 us -> 19.2 us
  starting transfers between devices: 96.7 us -> 80.9 us
  Pallas kernels: 89.2 us -> 99.6 us
  local copies, waits for them, and re-layouts: 22.3 us -> 13.8 us
    all_gather x4, waiting for transfers between devices: 78.2 us -> 0.06 us  [on_device(): near_own = [lax.all_gather(v, 'x', axis=0, tiled=True) for v in nears]]
    all_to_all x0 -> x2, blocking collectives: none -> 19.2 us  [over_x(): return lax.all_to_all(value, 'x', 0, 0)]
    ppermute x15 -> x3, starting transfers between devices: 17.8 us -> 3.89 us  [on_device(): lax.ppermute(code_late, 'x', xor_pairs(4, k))]
    all_to_all x0 -> x2, waiting for transfers between devices: none -> 11.1 us  [over_x(): return lax.all_to_all(value, 'x', 0, 0)]
    pallas_call x18 -> x21, Pallas kernels: 89.2 us -> 99.6 us  [call(): pl.pallas_call(kernel, out_shape=outs, in_specs=[pl.BlockSpec(memory_spac...]
    ppermute x6, waiting for transfers between devices: 2.62 us -> 12.6 us  [direct_gather(): lax.ppermute(v, axis, xor_pairs(4, k))]
    unnamed x70 -> x72, local copies, waits for them, and re-layouts: 17.5 us -> 8.15 us
    ppermute x15 -> x3, waiting for transfers between devices: 11.7 us -> 4.01 us  [on_device(): lax.ppermute(code_late, 'x', xor_pairs(4, k))]
  transfers between devices with their start and end apart: 49 -> 39, of which waited for: 18 -> 15; matrix products, arithmetic and copies ran while one was open for 5% -> 7% of each run, Pallas kernels for 18% -> 31%
where the time goes in v3:
time: 303 us; the launch traced here: 301 us
  Pallas kernels  99.6 us (33%)
  starting transfers between devices  80.9 us (27%)
  waiting for transfers between devices  53.6 us (18%)
  blocking collectives  19.2 us (6%)
  between operations  17.9 us (6%)
  other arithmetic  14.7 us (5%)
  local copies, waits for them, and re-layouts  13.8 us (5%)
    pallas_call x21, Pallas kernels, call(): pl.pallas_call(kernel, out_shape=outs, in_specs=[pl.BlockSpec(memory_spac...  99.6 us
    all_to_all x6, starting transfers between devices, on_device(): solved = lax.all_to_all(sent, ('z', 'y'), 0, 0).reshape(32, half, block)  30.7 us
    ppermute x10, starting transfers between devices, swap_cores(): return lax.ppermute(v, 'core', xor_pairs(2, 1))  19.4 us
    all_to_all x2, blocking collectives, over_x(): return lax.all_to_all(value, 'x', 0, 0)  19.2 us
    ppermute x2, waiting for transfers between devices, ring_gather(): before = lax.ppermute(v, axis, shift_pairs(4, 1))  13.2 us
    ppermute x6, waiting for transfers between devices, direct_gather(): lax.ppermute(v, axis, xor_pairs(4, k))  12.6 us
    all_to_all x2, waiting for transfers between devices, over_x(): return lax.all_to_all(value, 'x', 0, 0)  11.1 us
    ppermute x6, starting transfers between devices, direct_gather(): lax.ppermute(v, axis, xor_pairs(4, k))  9.2 us
  transfers between devices with their start and end apart: 39, of which 15 were waited for; matrix products, arithmetic and copies ran while one was open for 7% of the time, Pallas kernels for 31%

profile of v3, /device:TPU:1, one launch (start us, length us, event | category | flops | bytes accessed | tf_op | source)
XLA Modules:
  0.0 300.6 jit_solution(11031208366061113839)
XLA Ops:
  22.1 6.0 %collective-permute-done.3 = bf16[17,32,128]{2,1,0:T(8,128)(2,1)S(1)} collective-permute-done((bf16[17,32,128]{2,1,0:T(8,128)(2,1)S(1)}, bf16[17,32,128]{2,1,0:T(8,128)(2,1)S(1)}, u32[]{:S(2)}, u32[]{:S(2)}) %collective-permute-start.3) | collective-permute-done | bytes 139296 | tf_op jit(solution)/shard_map/ppermute | solution.py:27
  34.1 11.6 %collective-permute-done.5.refs_1_ = bf16[68,32,128]{2,1,0:T(8,128)(2,1)S(1)} collective-permute-done((bf16[68,32,128]{2,1,0:T(8,128)(2,1)S(1)}, bf16[68,32,128]{2,1,0:T(8,128)(2,1)S(1)}, u32[]{:S(2)}, u32[]{:S(2)}) %collective-permute-start.5) | collective-permute-done | bytes 557088 | tf_op jit(solution)/shard_map/ppermute | solution.py:31
  95.0 6.0 %first_sums.1 = (f32[4,2,2,32,128]{4,3,2,1,0:T(8,128)S(1)}, bf16[2048,32,128]{2,1,0:T(8,128)(2,1)}) custom-call(s32[7,64]{1,0:T(8,128)S(1)} %fusion.112.code_ref, s32[1]{0:T(128)} %bitcast.70.flag_ref, bf16[68,32,128]{2,1,0:T(8,128)(2,1)S(1)} %constant_dynamic-update-slice_fusion.14.refs_0_, bf16[68,32,128]{2,1,0:T(8,128)(2,1)S(1)} %collective-permute-done.5.refs_1_, ...), custom_call_target="tpu_custom_call" | custom-call | flops 134217728 | bytes 12582912 | tf_op jit(solution)/shard_map/first_sums/pallas_call | solution.py:60
  101.7 6.6 %collective-permute-start.22 = (bf16[88,128,128]{2,1,0:T(8,128)(2,1)}, bf16[88,128,128]{2,1,0:T(8,128)(2,1)}, u32[]{:S(2)}, u32[]{:S(2)}) collective-permute-start(bf16[88,128,128]{2,1,0:T(8,128)(2,1)} %all-gather.15.cloned.1.call-done.refs_0_.refs_1_), channel_id=1, source_target_pairs={{0,4},{4,0},{1,5},{5,1},{2,6},{6,2},{3,7},{7,3},{8,12},{12,8},{9,1... | collective-permute-start | bytes 8650760 | tf_op jit(solution)/shard_map/ppermute | solution.py:23
  109.1 4.2 %collective-permute-done.20 = bf16[8,1,32,128]{3,2,1,0:T(8,128)(2,1)S(1)} collective-permute-done((bf16[8,1,32,128]{3,2,1,0:T(8,128)(2,1)S(1)}, bf16[8,1,32,128]{3,2,1,0:T(8,128)(2,1)S(1)}, u32[]{:S(2)}, u32[]{:S(2)}) %collective-permute-start.20) | collective-permute-done | bytes 65568 | tf_op jit(solution)/shard_map/ppermute | solution.py:23
  118.3 6.9 %all-to-all-done.refs_0_.refs_5_ = f32[4,2,2,32,128]{4,3,2,1,0:T(8,128)S(1)} async-done(((f32[4,2,2,32,128]{4,3,2,1,0:T(8,128)}), f32[4,2,2,32,128]{4,3,2,1,0:T(8,128)S(1)}, u32[]{:S(2)}, u32[]{:S(2)}) %all-to-all-start) | async-done | bytes 262176 | tf_op jit(solution)/shard_map/all_to_all | solution.py:465
  128.7 6.6 %all-to-all-start.1 = ((bf16[16,2,32,128]{3,2,1,0:T(8,128)(2,1)}), bf16[16,2,32,128]{3,2,1,0:T(8,128)(2,1)S(1)}, u32[]{:S(2)}, u32[]{:S(2)}) async-start(bf16[16,2,32,128]{3,2,1,0:T(8,128)(2,1)} %get-tuple-element.186), calls=%async_computation.1 | async-start | bytes 524288 | tf_op jit(solution)/shard_map/all_to_all | solution.py:482
  138.3 7.6 %known_sums.3 = f32[4,2,2,32,128]{4,3,2,1,0:T(8,128)} custom-call(s32[7,64]{1,0:T(8,128)} %copy-done.1, bf16[2048,32,128]{2,1,0:T(8,128)(2,1)} %get-tuple-element.188.store_ref, bf16[7,1,32,128,128]{4,3,2,1,0:T(8,128)(2,1)} %own_ref.5, bf16[7,1,32,128,128]{4,3,2,1,0:T(8,128)(2,1)} %collective-permute-done.19.refs_11_.other_ref), custom_call_target="tpu_custom_call" | custom-call | flops 134217728 | bytes 12582912 | tf_op jit(solution)/shard_map/known_sums/pallas_call | solution.py:60
  146.0 4.6 %middle_sum.6 = (f32[2,32,128]{2,1,0:T(8,128)}, bf16[48,128,128]{2,1,0:T(8,128)(2,1)}) custom-call(s32[2,14]{1,0:T(2,128)} %pad_add_fusion.2.counts_ref.refs_0_, s32[14,24]{1,0:T(8,128)} %fusion.102.fresh_ref.refs_1_, s32[14,52]{1,0:T(8,128)} %fusion.100.middle_ref, bf16[88,128,128]{2,1,0:T(8,128)(2,1)} %all-gather.15.cloned.1.call-done.refs_0_.refs_1_, ...), custom_call_target="tpu_custom_call" | custom-call | flops 41943040 | bytes 8388608 | tf_op jit(solution)/shard_map/middle_sum/pallas_call | solution.py:60
  150.6 4.0 %solve_level.8 = (bf16[2,32,128]{2,1,0:T(8,128)(2,1)}, bf16[16,2,32,128]{3,2,1,0:T(8,128)(2,1)}) custom-call(s32[2,14]{1,0:T(2,128)} %pad_add_fusion.2.counts_ref.refs_0_, s32[14,24]{1,0:T(8,128)} %fusion.102.fresh_ref.refs_1_, f32[2,32,128]{2,1,0:T(8,128)} %get-tuple-element.193.refs_2_, bf16[48,128,128]{2,1,0:T(8,128)(2,1)} %get-tuple-element.194.refs_3_, ...), custom_call_target="tpu_custom_call" | custom-call | tf_op jit(solution)/shard_map/solve_level/pallas_call | solution.py:60
  155.9 9.6 %all_to_all.50.refs_5_ = f32[4,2,2,32,128]{4,3,2,1,0:T(8,128)} all-to-all(f32[4,2,2,32,128]{4,3,2,1,0:T(8,128)S(1)} %copy-done.12), channel_id=1, replica_groups=mesh['z'=4,'y'=4,'core'=2,'x'=4] {'x'}, dimensions={0} | all-to-all | bytes 524288 | tf_op jit(solution)/shard_map/all_to_all | solution.py:465
  165.5 6.8 %all-to-all-start.2 = ((bf16[16,2,32,128]{3,2,1,0:T(8,128)(2,1)}), bf16[16,2,32,128]{3,2,1,0:T(8,128)(2,1)S(1)}, u32[]{:S(2)}, u32[]{:S(2)}) async-start(bf16[16,2,32,128]{3,2,1,0:T(8,128)(2,1)} %get-tuple-element.200), calls=%async_computation.2 | async-start | bytes 524288 | tf_op jit(solution)/shard_map/all_to_all | solution.py:482
  172.3 5.3 %middle_sum.7 = (f32[2,32,128]{2,1,0:T(8,128)}, bf16[48,128,128]{2,1,0:T(8,128)(2,1)}) custom-call(s32[2,14]{1,0:T(2,128)} %pad_add_fusion.2.counts_ref.refs_0_, s32[14,24]{1,0:T(8,128)} %fusion.102.fresh_ref.refs_1_, s32[14,52]{1,0:T(8,128)} %fusion.100.middle_ref, bf16[32,32,128]{2,1,0:T(8,128)(2,1)} %bitcast.220, ...), custom_call_target="tpu_custom_call" | custom-call | flops 41943040 | bytes 8388608 | tf_op jit(solution)/shard_map/middle_sum/pallas_call | solution.py:60
  180.6 4.2 %solve_level.9 = (bf16[2,32,128]{2,1,0:T(8,128)(2,1)}, bf16[16,2,32,128]{3,2,1,0:T(8,128)(2,1)}) custom-call(s32[2,14]{1,0:T(2,128)} %pad_add_fusion.2.counts_ref.refs_0_, s32[14,24]{1,0:T(8,128)} %fusion.102.fresh_ref.refs_1_, f32[2,32,128]{2,1,0:T(8,128)} %get-tuple-element.198.refs_2_, bf16[48,128,128]{2,1,0:T(8,128)(2,1)} %get-tuple-element.199.refs_3_, ...), custom_call_target="tpu_custom_call" | custom-call | tf_op jit(solution)/shard_map/solve_level/pallas_call | solution.py:60
  188.7 7.9 %known_sums.4 = f32[4,2,2,32,128]{4,3,2,1,0:T(8,128)} custom-call(s32[7,64]{1,0:T(8,128)} %copy-done.1, bf16[2048,32,128]{2,1,0:T(8,128)(2,1)} %get-tuple-element.188.store_ref, bf16[7,1,32,128,128]{4,3,2,1,0:T(8,128)(2,1)} %own_ref.5, bf16[7,1,32,128,128]{4,3,2,1,0:T(8,128)(2,1)} %collective-permute-done.19.refs_11_.other_ref), custom_call_target="tpu_custom_call" | custom-call | flops 134217728 | bytes 12582912 | tf_op jit(solution)/shard_map/known_sums/pallas_call | solution.py:60
  196.6 5.7 %middle_sum.8 = (f32[2,32,128]{2,1,0:T(8,128)}, bf16[48,128,128]{2,1,0:T(8,128)(2,1)}) custom-call(s32[2,14]{1,0:T(2,128)} %pad_add_fusion.2.counts_ref.refs_0_, s32[14,24]{1,0:T(8,128)} %fusion.102.fresh_ref.refs_1_, s32[14,52]{1,0:T(8,128)} %fusion.100.middle_ref, bf16[32,32,128]{2,1,0:T(8,128)(2,1)} %bitcast.221, bf16[32,32,128]{2,1,0:T(8,128)(2,1)} %bitcast.227, ...), custom_call_target="tpu_custom_call" | custom-call | flops 41943040 | bytes 8388608 | tf_op jit(solution)/shard_map/middle_sum/pallas_call | solution.py:60
  209.2 9.6 %all_to_all.51.refs_5_ = f32[4,2,2,32,128]{4,3,2,1,0:T(8,128)} all-to-all(f32[4,2,2,32,128]{4,3,2,1,0:T(8,128)S(1)} %copy-done.13), channel_id=1, replica_groups=mesh['z'=4,'y'=4,'core'=2,'x'=4] {'x'}, dimensions={0} | all-to-all | bytes 524288 | tf_op jit(solution)/shard_map/all_to_all | solution.py:465
  218.7 6.1 %all-to-all-start.5 = ((bf16[16,2,32,128]{3,2,1,0:T(8,128)(2,1)}), bf16[16,2,32,128]{3,2,1,0:T(8,128)(2,1)S(1)}, u32[]{:S(2)}, u32[]{:S(2)}) async-start(bf16[16,2,32,128]{3,2,1,0:T(8,128)(2,1)} %get-tuple-element.217), calls=%async_computation.5 | async-start | bytes 524288 | tf_op jit(solution)/shard_map/all_to_all | solution.py:482
  224.9 5.6 %middle_sum.9 = (f32[2,32,128]{2,1,0:T(8,128)}, bf16[48,128,128]{2,1,0:T(8,128)(2,1)}) custom-call(s32[2,14]{1,0:T(2,128)} %pad_add_fusion.2.counts_ref.refs_0_, s32[14,24]{1,0:T(8,128)} %fusion.102.fresh_ref.refs_1_, s32[14,52]{1,0:T(8,128)} %fusion.100.middle_ref, bf16[32,32,128]{2,1,0:T(8,128)(2,1)} %bitcast.222, bf16[32,32,128]{2,1,0:T(8,128)(2,1)} %bitcast.228, ...), custom_call_target="tpu_custom_call" | custom-call | flops 41943040 | bytes 8388608 | tf_op jit(solution)/shard_map/middle_sum/pallas_call | solution.py:60
  233.2 4.0 %solve_level.11 = (bf16[2,32,128]{2,1,0:T(8,128)(2,1)}, bf16[16,2,32,128]{3,2,1,0:T(8,128)(2,1)}) custom-call(s32[2,14]{1,0:T(2,128)} %pad_add_fusion.2.counts_ref.refs_0_, s32[14,24]{1,0:T(8,128)} %fusion.102.fresh_ref.refs_1_, f32[2,32,128]{2,1,0:T(8,128)} %get-tuple-element.215.refs_2_, bf16[48,128,128]{2,1,0:T(8,128)(2,1)} %get-tuple-element.216.refs_3_, ...), custom_call_target="tpu_custom_call" | custom-call | tf_op jit(solution)/shard_map/solve_level/pallas_call | solution.py:60
  243.7 5.1 %known_sums.5 = f32[4,1,2,32,128]{4,3,2,1,0:T(8,128)} custom-call(s32[7,64]{1,0:T(8,128)} %copy-done.1, bf16[2048,32,128]{2,1,0:T(8,128)(2,1)} %get-tuple-element.188.store_ref, bf16[7,1,32,128,128]{4,3,2,1,0:T(8,128)(2,1)} %own_ref.5, bf16[7,1,32,128,128]{4,3,2,1,0:T(8,128)(2,1)} %collective-permute-done.19.refs_11_.other_ref), custom_call_target="tpu_custom_call" | custom-call | flops 67108864 | bytes 6291456 | tf_op jit(solution)/shard_map/known_sums/pallas_call | solution.py:60
  252.1 6.1 %middle_sum.10 = (f32[2,32,128]{2,1,0:T(8,128)}, bf16[48,128,128]{2,1,0:T(8,128)(2,1)}) custom-call(s32[2,14]{1,0:T(2,128)} %pad_add_fusion.2.counts_ref.refs_0_, s32[14,24]{1,0:T(8,128)} %fusion.102.fresh_ref.refs_1_, s32[14,52]{1,0:T(8,128)} %fusion.100.middle_ref, bf16[32,32,128]{2,1,0:T(8,128)(2,1)} %bitcast.223, bf16[32,32,128]{2,1,0:T(8,128)(2,1)} %bitcast.229, ...), custom_call_target="tpu_custom_call" | custom-call | flops 41943040 | bytes 8388608 | tf_op jit(solution)/shard_map/middle_sum/pallas_call | solution.py:60
  266.1 4.2 %all-to-all-done.9.refs_5_ = f32[4,1,2,32,128]{4,3,2,1,0:T(8,128)S(1)} async-done(((f32[4,1,2,32,128]{4,3,2,1,0:T(8,128)}), f32[4,1,2,32,128]{4,3,2,1,0:T(8,128)S(1)}, u32[]{:S(2)}, u32[]{:S(2)}) %all-to-all-start.9) | async-done | bytes 131104 | tf_op jit(solution)/shard_map/all_to_all | solution.py:465
  277.2 6.7 %middle_sum.11 = (f32[2,32,128]{2,1,0:T(8,128)}, bf16[48,128,128]{2,1,0:T(8,128)(2,1)}) custom-call(s32[2,14]{1,0:T(2,128)} %pad_add_fusion.2.counts_ref.refs_0_, s32[14,24]{1,0:T(8,128)} %fusion.102.fresh_ref.refs_1_, s32[14,52]{1,0:T(8,128)} %fusion.100.middle_ref, bf16[32,32,128]{2,1,0:T(8,128)(2,1)} %bitcast.224, bf16[32,32,128]{2,1,0:T(8,128)(2,1)} %bitcast.230, ...), custom_call_target="tpu_custom_call" | custom-call | flops 41943040 | bytes 8388608 | tf_op jit(solution)/shard_map/middle_sum/pallas_call | solution.py:60
  (213 shorter events, 131.6 us)
Async XLA Ops:
  7.4 94.3 %all-gather.15.cloned.1.call-start = ((), (), s32[]{:S(2)}) async-start(), calls=%async_computation.11 | async-start | bytes 3604480 | tf_op jit(solution)/shard_map/all_gather | solution.py:407
  18.0 10.1 %collective-permute-start.3 = (bf16[17,32,128]{2,1,0:T(8,128)(2,1)S(1)}, bf16[17,32,128]{2,1,0:T(8,128)(2,1)S(1)}, u32[]{:S(2)}, u32[]{:S(2)}) collective-permute-start(bf16[17,32,128]{2,1,0:T(8,128)(2,1)S(1)} %get-tuple-element.178), channel_id=1, source_target_pairs={{0,64},{32,96},{64,0},{96,32},{1,65},{33,97},{65,1},{97,33},{2,66}... | collective-permute-start | bytes 417800 | tf_op jit(solution)/shard_map/ppermute | solution.py:27
  21.4 73.5 %collective-permute-start.19 = (bf16[7,1,32,128,128]{4,3,2,1,0:T(8,128)(2,1)}, bf16[7,1,32,128,128]{4,3,2,1,0:T(8,128)(2,1)}, u32[]{:S(2)}, u32[]{:S(2)}) collective-permute-start(bf16[7,1,32,128,128]{4,3,2,1,0:T(8,128)(2,1)} %own_ref.5), channel_id=1, source_target_pairs={{0,4},{4,0},{1,5},{5,1},{2,6},{6,2},{3,7},{7,3},{8,12},{12,8},{9,1... | collective-permute-start | bytes 22020104 | tf_op jit(solution)/shard_map/ppermute | solution.py:23
  30.8 14.9 %collective-permute-start.5 = (bf16[68,32,128]{2,1,0:T(8,128)(2,1)S(1)}, bf16[68,32,128]{2,1,0:T(8,128)(2,1)S(1)}, u32[]{:S(2)}, u32[]{:S(2)}) collective-permute-start(bf16[68,32,128]{2,1,0:T(8,128)(2,1)S(1)} %constant_dynamic-update-slice_fusion.14.refs_0_), channel_id=1, source_target_pairs={{0,8},{8,16},{16,24},{24,0},{1,9},{9,17},{17,25},{25,1},{2,10},{10... | collective-permute-start | bytes 1671176 | tf_op jit(solution)/shard_map/ppermute | solution.py:31
  59.5 95.2 %all-gather.17.cloned.1.call-start = ((), (), s32[]{:S(2)}) async-start(), calls=%async_computation.12 | async-start | bytes 4915200 | tf_op jit(solution)/shard_map/all_gather | solution.py:407
  63.4 142.9 %all-gather.19.cloned.1.call-start = ((), (), s32[]{:S(2)}) async-start(), calls=%async_computation.13 | async-start | bytes 2785280 | tf_op jit(solution)/shard_map/all_gather | solution.py:407
  71.5 11.3 %collective-permute-start.15 = (bf16[68,32,128]{2,1,0:T(8,128)(2,1)S(1)}, bf16[68,32,128]{2,1,0:T(8,128)(2,1)S(1)}, u32[]{:S(2)}, u32[]{:S(2)}) collective-permute-start(bf16[68,32,128]{2,1,0:T(8,128)(2,1)S(1)} %constant_dynamic-update-slice_fusion.18.refs_5_), channel_id=1, source_target_pairs={{0,32},{32,64},{64,96},{96,0},{1,33},{33,65},{65,97},{97,1},{2,34}... | collective-permute-start | bytes 1671176 | tf_op jit(solution)/shard_map/ppermute | solution.py:31
  71.6 12.0 %collective-permute-start.16 = (bf16[68,32,128]{2,1,0:T(8,128)(2,1)S(1)}, bf16[68,32,128]{2,1,0:T(8,128)(2,1)S(1)}, u32[]{:S(2)}, u32[]{:S(2)}) collective-permute-start(bf16[68,32,128]{2,1,0:T(8,128)(2,1)S(1)} %constant_dynamic-update-slice_fusion.18.refs_5_), channel_id=1, source_target_pairs={{0,96},{32,0},{64,32},{96,64},{1,97},{33,1},{65,33},{97,65},{2,98}... | collective-permute-start | bytes 1671176 | tf_op jit(solution)/shard_map/ppermute | solution.py:32
  74.3 13.4 %collective-permute-start.9 = (bf16[68,32,128]{2,1,0:T(8,128)(2,1)S(1)}, bf16[68,32,128]{2,1,0:T(8,128)(2,1)S(1)}, u32[]{:S(2)}, u32[]{:S(2)}) collective-permute-start(bf16[68,32,128]{2,1,0:T(8,128)(2,1)S(1)} %constant_dynamic-update-slice_fusion.14.refs_0_), channel_id=1, source_target_pairs={{0,24},{8,0},{16,8},{24,16},{1,25},{9,1},{17,9},{25,17},{2,26},{10... | collective-permute-start | bytes 1671176 | tf_op jit(solution)/shard_map/ppermute | solution.py:32
  83.6 11.3 %collective-permute-start.17 = (bf16[34,32,128]{2,1,0:T(8,128)(2,1)}, bf16[34,32,128]{2,1,0:T(8,128)(2,1)}, u32[]{:S(2)}, u32[]{:S(2)}) collective-permute-start(bf16[34,32,128]{2,1,0:T(8,128)(2,1)} %slice.383), channel_id=1, source_target_pairs={{0,32},{32,64},{64,96},{96,0},{1,33},{33,65},{65,97},{97,1},{2,34}... | collective-permute-start | bytes 835592 | tf_op jit(solution)/shard_map/ppermute | solution.py:34
  84.3 10.6 %collective-permute-start.18 = (bf16[34,32,128]{2,1,0:T(8,128)(2,1)}, bf16[34,32,128]{2,1,0:T(8,128)(2,1)}, u32[]{:S(2)}, u32[]{:S(2)}) collective-permute-start(bf16[34,32,128]{2,1,0:T(8,128)(2,1)} %slice.384), channel_id=1, source_target_pairs={{0,96},{32,0},{64,32},{96,64},{1,97},{33,1},{65,33},{97,65},{2,98}... | collective-permute-start | bytes 835592 | tf_op jit(solution)/shard_map/ppermute | solution.py:35
  101.7 44.2 %collective-permute-start.22 = (bf16[88,128,128]{2,1,0:T(8,128)(2,1)}, bf16[88,128,128]{2,1,0:T(8,128)(2,1)}, u32[]{:S(2)}, u32[]{:S(2)}) collective-permute-start(bf16[88,128,128]{2,1,0:T(8,128)(2,1)} %all-gather.15.cloned.1.call-done.refs_0_.refs_1_), channel_id=1, source_target_pairs={{0,4},{4,0},{1,5},{5,1},{2,6},{6,2},{3,7},{7,3},{8,12},{12,8},{9,1... | collective-permute-start | bytes 8650760 | tf_op jit(solution)/shard_map/ppermute | solution.py:23
  108.5 9.8 %collective-permute-start.21 = (bf16[8,1,128,128]{3,2,1,0:T(8,128)(2,1)}, bf16[8,1,128,128]{3,2,1,0:T(8,128)(2,1)S(1)}, u32[]{:S(2)}, u32[]{:S(2)}) collective-permute-start(bf16[8,1,128,128]{3,2,1,0:T(8,128)(2,1)} %refs_7_.11), channel_id=1, source_target_pairs={{0,4},{4,0},{1,5},{5,1},{2,6},{6,2},{3,7},{7,3},{8,12},{12,8},{9,1... | collective-permute-start | bytes 786440 | tf_op jit(solution)/shard_map/ppermute | solution.py:23
  114.0 11.2 %all-to-all-start = ((f32[4,2,2,32,128]{4,3,2,1,0:T(8,128)}), f32[4,2,2,32,128]{4,3,2,1,0:T(8,128)S(1)}, u32[]{:S(2)}, u32[]{:S(2)}) async-start(f32[4,2,2,32,128]{4,3,2,1,0:T(8,128)} %copy-done), calls=%async_computation | async-start | bytes 524288 | tf_op jit(solution)/shard_map/all_to_all | solution.py:465
  128.7 17.2 %all-to-all-start.1 = ((bf16[16,2,32,128]{3,2,1,0:T(8,128)(2,1)}), bf16[16,2,32,128]{3,2,1,0:T(8,128)(2,1)S(1)}, u32[]{:S(2)}, u32[]{:S(2)}) async-start(bf16[16,2,32,128]{3,2,1,0:T(8,128)(2,1)} %get-tuple-element.186), calls=%async_computation.1 | async-start | bytes 524288 | tf_op jit(solution)/shard_map/all_to_all | solution.py:482
  135.3 101.9 %all-gather.21.cloned.1.call-start = ((), (), s32[]{:S(2)}) async-start(), calls=%async_computation.14 | async-start | bytes 2949120 | tf_op jit(solution)/shard_map/all_gather | solution.py:407
  154.7 41.9 %collective-permute-start.23 = (bf16[120,128,128]{2,1,0:T(8,128)(2,1)}, bf16[120,128,128]{2,1,0:T(8,128)(2,1)}, u32[]{:S(2)}, u32[]{:S(2)}) collective-permute-start(bf16[120,128,128]{2,1,0:T(8,128)(2,1)} %all-gather.17.cloned.1.call-done.refs_2_.refs_3_), channel_id=1, source_target_pairs={{0,4},{4,0},{1,5},{5,1},{2,6},{6,2},{3,7},{7,3},{8,12},{12,8},{9,1... | collective-permute-start | bytes 11796488 | tf_op jit(solution)/shard_map/ppermute | solution.py:23
  165.5 14.4 %all-to-all-start.2 = ((bf16[16,2,32,128]{3,2,1,0:T(8,128)(2,1)}), bf16[16,2,32,128]{3,2,1,0:T(8,128)(2,1)S(1)}, u32[]{:S(2)}, u32[]{:S(2)}) async-start(bf16[16,2,32,128]{3,2,1,0:T(8,128)(2,1)} %get-tuple-element.200), calls=%async_computation.2 | async-start | bytes 524288 | tf_op jit(solution)/shard_map/all_to_all | solution.py:482
  184.8 11.8 %all-to-all-start.4 = ((bf16[16,2,32,128]{3,2,1,0:T(8,128)(2,1)}), bf16[16,2,32,128]{3,2,1,0:T(8,128)(2,1)S(1)}, u32[]{:S(2)}, u32[]{:S(2)}) async-start(bf16[16,2,32,128]{3,2,1,0:T(8,128)(2,1)} %get-tuple-element.209), calls=%async_computation.4 | async-start | bytes 524288 | tf_op jit(solution)/shard_map/all_to_all | solution.py:482
  206.3 45.8 %collective-permute-start.24 = (bf16[68,128,128]{2,1,0:T(8,128)(2,1)}, bf16[68,128,128]{2,1,0:T(8,128)(2,1)}, u32[]{:S(2)}, u32[]{:S(2)}) collective-permute-start(bf16[68,128,128]{2,1,0:T(8,128)(2,1)} %all-gather.19.cloned.1.call-done.refs_4_), channel_id=1, source_target_pairs={{0,4},{4,0},{1,5},{5,1},{2,6},{6,2},{3,7},{7,3},{8,12},{12,8},{9,1... | collective-permute-start | bytes 6684680 | tf_op jit(solution)/shard_map/ppermute | solution.py:23
  218.7 13.7 %all-to-all-start.5 = ((bf16[16,2,32,128]{3,2,1,0:T(8,128)(2,1)}), bf16[16,2,32,128]{3,2,1,0:T(8,128)(2,1)S(1)}, u32[]{:S(2)}, u32[]{:S(2)}) async-start(bf16[16,2,32,128]{3,2,1,0:T(8,128)(2,1)} %get-tuple-element.217), calls=%async_computation.5 | async-start | bytes 524288 | tf_op jit(solution)/shard_map/all_to_all | solution.py:482
  237.2 38.6 %collective-permute-start.25 = (bf16[72,128,128]{2,1,0:T(8,128)(2,1)}, bf16[72,128,128]{2,1,0:T(8,128)(2,1)S(1)}, u32[]{:S(2)}, u32[]{:S(2)}) collective-permute-start(bf16[72,128,128]{2,1,0:T(8,128)(2,1)} %all-gather.21.cloned.1.call-done.refs_5_), channel_id=1, source_target_pairs={{0,4},{4,0},{1,5},{5,1},{2,6},{6,2},{3,7},{7,3},{8,12},{12,8},{9,1... | collective-permute-start | bytes 7077896 | tf_op jit(solution)/shard_map/ppermute | solution.py:23
  239.8 12.3 %all-to-all-start.7 = ((bf16[16,2,32,128]{3,2,1,0:T(8,128)(2,1)}), bf16[16,2,32,128]{3,2,1,0:T(8,128)(2,1)S(1)}, u32[]{:S(2)}, u32[]{:S(2)}) async-start(bf16[16,2,32,128]{3,2,1,0:T(8,128)(2,1)} %get-tuple-element.226), calls=%async_computation.7 | async-start | bytes 524288 | tf_op jit(solution)/shard_map/all_to_all | solution.py:482
  270.3 13.6 %all-to-all-start.8 = ((bf16[16,2,32,128]{3,2,1,0:T(8,128)(2,1)}), bf16[16,2,32,128]{3,2,1,0:T(8,128)(2,1)S(1)}, u32[]{:S(2)}, u32[]{:S(2)}) async-start(bf16[16,2,32,128]{3,2,1,0:T(8,128)(2,1)} %get-tuple-element.235), calls=%async_computation.8 | async-start | bytes 524288 | tf_op jit(solution)/shard_map/all_to_all | solution.py:482
  (46 other events, 756.0 us)
Sparse Core Ops, SparseCore 0:
  16.3 39.5 all-gather.14
  63.5 43.0 all-gather.16
  108.5 34.0 all-gather.18
  156.0 32.3 all-gather.20
Sparse Core Ops, SparseCore 1:
  59.0 2.5 sort.21.cloned.1.call-done
  63.9 2.5 sort.23.cloned.1.call-done
  (2 shorter events, 0.0 us)
